TPU v7x, 1024 devices: a whole 4x4x32 slice. The times are simulated.
1024 devices in a mesh: dp: 16 (over z_hi, x), expert: 8 (over z_lo), tensor: 8 (over y, core).
Axes of the slice: x: 4, y: 4, z: 32 (z_hi: 4, z_lo: 8; z = z_hi * 8 + z_lo), core: 2. Of those that a mesh axis runs over, the one named last changes fastest.
Arguments:
- tokens: bfloat16 [768, 3072], P('expert', 'tensor'), may hold values from -6 to 6
- cotangent: bfloat16 [768, 3072], P('expert', 'tensor'), may hold values from -6 to 6
- expert_ids: int32 [768, 2], P('expert'), may hold values from 0 to 7, all different within a row; in each aligned block of 96 rows (0 to 95, 96 to 191, ...) at most 32 rows name the same one
- gate_probs: bfloat16 [768, 2], P('expert'), may hold values from 0.049804688 to 0.94921875
- tenant_ids: int32 [768], P('expert'), may hold values from 0 to 7
- w_gate: bfloat16 [8, 3072, 16384], P('expert', None, ('dp', 'tensor')), may hold values from -0.109375 to 0.109375
- w_up: bfloat16 [8, 3072, 16384], P('expert', None, ('dp', 'tensor')), may hold values from -0.109375 to 0.109375
- w_down: bfloat16 [8, 16384, 3072], P('expert', ('dp', 'tensor')), may hold values from -0.046875 to 0.046875
- adapter_in: bfloat16 [8, 16384, 128], P('expert', ('dp', 'tensor')), may hold values from -0.046875 to 0.046875
- adapter_out: bfloat16 [8, 128, 3072], P('expert'), may hold values from -0.109375 to 0.109375
Outputs:
- input_grad: bfloat16 [768, 3072], P('expert', ('dp', 'tensor'))
- grad_in: float32 [8, 16384, 128], P('expert', ('dp', 'tensor'))
- grad_out: float32 [8, 128, 3072], P('expert', None, 'tensor')
Inputs may be any that keep to these rules, and one draw needn't show every extreme that they name: `expert_ids`: the two experts of a token differ. Among the 96 tokens of each group (aligned blocks of the token rows of one index of expert), no expert is named more than 32 times, and in every draw some expert is named exactly 32 times in some group.
All inputs are finite; a program needn't handle non-finite values.
Results may differ from a plain program's by a relative error of at most 0.005.
Values may be sent and summed in bfloat16 or wider, within the bound.
No kernel may reach another device: no remote copies, remote signals or barrier semaphores. Data moves between devices by JAX's collectives and lax.ppermute only.
A program may use at most 32 MiB of HBM per device.

v0:
```python
import jax
import jax.numpy as jnp
from jax import lax
from jax.sharding import PartitionSpec as P

TEN = 8
RANK = 16
TOP = 2
CAP = 32


adapter_scale_factor = 2.0


def on_device(
    tokens,
    cotangent,
    expert_ids,
    gate_probs,
    tenant_ids,
    w_gate,
    w_up,
    w_down,
    adapter_in,
    adapter_out,
):
    experts = lax.axis_size("expert")
    tok_rows = tokens.shape[0]
    col_width = tokens.shape[1]
    slot_count = experts * CAP
    route_ids = expert_ids.reshape(-1)
    route_total = route_ids.shape[0]
    onehot = (route_ids[:, None] == jnp.arange(experts, dtype=jnp.int32)[None, :]).astype(jnp.int32)
    earlier = jnp.cumsum(onehot, axis=0) - onehot
    slot_index = jnp.sum(earlier * onehot, axis=1)
    target = route_ids * CAP + slot_index
    owner_token = jnp.arange(route_total, dtype=jnp.int32) // TOP
    slot_hits = (target[None, :] == jnp.arange(slot_count, dtype=jnp.int32)[:, None]).astype(
        jnp.float32
    )
    token_hits = (owner_token[:, None] == jnp.arange(tok_rows, dtype=jnp.int32)[None, :]).astype(
        jnp.float32
    )
    dispatch = jnp.dot(slot_hits, token_hits, precision=lax.Precision.HIGHEST)
    tenant_hot = (tenant_ids[:, None] == jnp.arange(TEN, dtype=jnp.int32)[None, :]).astype(
        jnp.float32
    )
    route_weight = gate_probs.reshape(-1).astype(jnp.float32)
    route_marks = (
        jnp.dot(token_hits, tenant_hot, precision=lax.Precision.HIGHEST) * route_weight[:, None]
    )
    slot_marks = jnp.dot(slot_hits, route_marks, precision=lax.Precision.HIGHEST)
    dispatch_half = dispatch.astype(jnp.bfloat16)
    send_inputs = jnp.dot(dispatch_half, tokens, preferred_element_type=jnp.float32).astype(
        jnp.bfloat16
    )
    send_grads = jnp.dot(dispatch_half, cotangent, preferred_element_type=jnp.float32).astype(
        jnp.bfloat16
    )
    send_inputs = send_inputs.reshape(experts, CAP, col_width)
    send_grads = send_grads.reshape(experts, CAP, col_width)
    send_marks = slot_marks.astype(jnp.bfloat16).reshape(experts, CAP, TEN)
    recv_inputs, recv_grads, recv_marks = (
        lax.all_to_all(send_inputs, "expert", split_axis=0, concat_axis=0, tiled=True),
        lax.all_to_all(send_grads, "expert", split_axis=0, concat_axis=0, tiled=True),
        lax.all_to_all(send_marks, "expert", split_axis=0, concat_axis=0, tiled=True),
    )
    gate_mat = w_gate[0]
    up_mat = w_up[0]
    down_mat = w_down[0]
    first_factor = adapter_in[0]
    second_factor = adapter_out[0]
    hidden_units = gate_mat.shape[1]
    low_width = first_factor.shape[1]
    input_piece = lax.all_gather(recv_inputs, "tensor", axis=2, tiled=True)
    grad_piece = lax.all_gather(recv_grads, "tensor", axis=2, tiled=True)
    piece_width = input_piece.shape[2]
    input_piece = input_piece.reshape(slot_count, piece_width)
    grad_piece = grad_piece.reshape(slot_count, piece_width)
    gate_rows = gate_mat
    up_projection_rows = up_mat
    gate_acc = jnp.dot(input_piece, gate_rows, preferred_element_type=jnp.float32)
    up_acc = jnp.dot(input_piece, up_projection_rows, preferred_element_type=jnp.float32)
    back_acc = lax.dot_general(
        grad_piece, down_mat, (((1,), (1,)), ((), ())), preferred_element_type=jnp.float32
    )
    low_acc = lax.dot_general(
        grad_piece, second_factor, (((1,), (1,)), ((), ())), preferred_element_type=jnp.float32
    )
    sig = jax.nn.sigmoid(gate_acc)
    silu_val = gate_acc * sig
    hidden = (silu_val * up_acc).astype(jnp.bfloat16)
    low_part = jnp.dot(hidden, first_factor, preferred_element_type=jnp.float32)
    marks_value = recv_marks.reshape(slot_count, TEN).astype(jnp.float32)
    row_weight = jnp.sum(marks_value, axis=1)
    broadcast_routing_flags = jnp.repeat(marks_value, RANK, axis=1)
    low_in = lax.psum(low_part, ("dp", "tensor"))
    gate_weighted_rows = adapter_scale_factor * broadcast_routing_flags
    down_coef = (gate_weighted_rows * low_acc).astype(jnp.bfloat16)
    up_coef = (gate_weighted_rows * low_in).astype(jnp.bfloat16)
    hidden_gradient = row_weight[:, None] * back_acc + lax.dot_general(
        down_coef, first_factor, (((1,), (1,)), ((), ())), preferred_element_type=jnp.float32
    )
    slope = sig * (1.0 + gate_acc * (1.0 - sig))
    gate_grad = (hidden_gradient * up_acc * slope).astype(jnp.bfloat16)
    up_grad = (hidden_gradient * silu_val).astype(jnp.bfloat16)
    grad_a = lax.dot_general(
        hidden, down_coef, (((0,), (0,)), ((), ())), preferred_element_type=jnp.float32
    )
    local_grads = recv_grads.reshape(slot_count, col_width)
    grad_b = lax.dot_general(
        up_coef, local_grads, (((0,), (0,)), ((), ())), preferred_element_type=jnp.float32
    )
    gate_rows = gate_mat
    up_projection_rows = up_mat
    term = lax.dot_general(
        gate_rows, gate_grad, (((1,), (1,)), ((), ())), preferred_element_type=jnp.float32
    )
    slices = lax.psum_scatter(
        term
        + lax.dot_general(
            up_projection_rows,
            up_grad,
            (((1,), (1,)), ((), ())),
            preferred_element_type=jnp.float32,
        ),
        ("dp", "tensor"),
        scatter_dimension=0,
        tiled=True,
    )
    slice_width = slices.shape[0]
    returned = lax.all_to_all(
        slices.reshape(slice_width, experts, CAP), "expert", split_axis=1, concat_axis=1, tiled=True
    )
    returned = returned.reshape(slice_width, slot_count)
    token_grad = lax.dot_general(
        dispatch,
        returned,
        (((0,), (1,)), ((), ())),
        precision=lax.Precision.HIGHEST,
        preferred_element_type=jnp.float32,
    )
    input_grad = token_grad.astype(jnp.bfloat16)
    return (
        input_grad,
        grad_a.reshape(1, hidden_units, low_width),
        grad_b.reshape(1, low_width, col_width),
    )


def solution(mesh):
    placed = (
        P("expert", "tensor"),
        P("expert", "tensor"),
        P("expert", None),
        P("expert", None),
        P("expert"),
        P("expert", None, ("dp", "tensor")),
        P("expert", None, ("dp", "tensor")),
        P("expert", ("dp", "tensor"), None),
        P("expert", ("dp", "tensor"), None),
        P("expert", None, None),
    )
    return jax.shard_map(
        on_device,
        mesh=mesh,
        in_specs=placed,
        out_specs=(
            P("expert", ("dp", "tensor")),
            P("expert", ("dp", "tensor"), None),
            P("expert", None, "tensor"),
        ),
        check_vma=False,
    )
```

profile of v0, /device:TPU:32, one launch (start us, length us, event | category | flops | bytes accessed | tf_op | source)
XLA Modules:
  0.0 2489.1 jit_solution(12072008702473450030)
XLA Ops:
  7.2 0.8 copy.23
  8.1 0.1 reshape.91
  8.3 0.6 reduce-window.6
  8.8 0.2 slice_reduce_fusion
  9.1 0.1 add_bitcast_fusion
  9.2 0.3 fusion.12
  9.5 1.1 convolution_convert_fusion
  10.6 25.9 %all_to_all.20 = bf16[8,32,384]{2,1,0:T(8,128)(2,1)} all-to-all(bf16[8,32,384]{2,1,0:T(8,128)(2,1)S(1)} %bitcast.73), channel_id=1, replica_groups=mesh['dp'=16,'expert'=8,'tensor'=8] {'expert'}, dimensions={0} | all-to-all | bytes 393216 | tf_op jit(solution)/shard_map/all_to_all | solution.py:64
  36.6 1.1 convolution_convert_fusion.1
  37.8 16.0 all_to_all.21
  53.8 0.0 reduce-scatter.4.cloned.1.call-start
  53.9 0.1 copy.24
  54.0 0.1 reshape.105
  54.2 0.3 convolution_multiply_fusion.2
  54.4 0.2 convolution_convert_fusion.3
  54.6 0.2 reshape.94
  54.8 0.1 reshape.109
  54.9 14.7 all_to_all.22
  69.6 0.1 reshape.110
  69.7 0.1 mul.76
  69.8 0.1 mul.81
  69.9 0.1 copy.27
  70.0 9.6 all-gather.5.cloned.1.call-done
  79.6 2.1 fusion.5
  81.7 1.2 multiply_convert_fusion.1
  83.0 42.0 %all-gather.3.cloned.1.call-done = bf16[8,32,3072]{2,1,0:T(8,128)(2,1)} async-done(((bf16[8,32,384]{2,1,0:T(8,128)(2,1)}), bf16[8,32,3072]{2,1,0:T(8,128)(2,1)}) %all-gather.3.cloned.1.call-update) | async-done | bytes 1572880 | tf_op jit(solution)/shard_map/all_gather | solution.py:76
  125.0 2.1 fusion.2
  127.1 0.2 fusion.21
  127.3 0.6 fusion.1
  127.9 0.1 copy-done.10
  128.1 0.6 fusion.3
  128.6 2.3 fusion
  130.9 3.5 copy.31
  134.5 0.8 copy-done.9
  135.3 0.8 fusion.19
  136.1 334.1 %reduce-scatter.4.cloned.1.call-done = f32[24,256]{1,0:T(8,128)} async-done(((f32[3072,256]{1,0:T(8,128)}), f32[24,256]{1,0:T(8,128)}) %reduce-scatter.4.cloned.1.call-update) | async-done | bytes 24592
  470.2 0.8 copy.32
  471.1 0.1 copy.28
  471.2 0.7 reshape.111
  471.9 8.4 all-to-all-start.3
  480.3 0.8 convolution_bitcast_fusion.1
  481.2 1997.4 %all-reduce.3.cloned.1.call-done = f32[256,128]{1,0:T(8,128)} async-done(((f32[256,128]{1,0:T(8,128)}), f32[256,128]{1,0:T(8,128)}) %all-reduce.3.cloned.1.call-update) | async-done | bytes 131088 | tf_op jit(solution)/shard_map/psum | solution.py:97
  2478.5 1.8 convolution_bitcast_fusion
  2480.3 0.5 broadcast.70
  2480.8 0.7 reduce.3
  2481.5 0.1 reshape.112
  2481.6 0.1 reshape.100
  2481.7 0.8 convolution_convert_fusion.2
  (45 shorter events, 0.4 us)
Async XLA Ops:
  7.2 74.5 %copy-start = (bf16[1,3072,128]{2,1,0:T(8,128)(2,1)S(1)}, bf16[1,3072,128]{2,1,0:T(8,128)(2,1)}, u32[]{:S(2)}) copy-start(bf16[1,3072,128]{2,1,0:T(8,128)(2,1)} %param.16) | copy-start | bytes 2359300
  7.2 46.7 %copy-start.12 = (bf16[96,2]{0,1:T(2,128)(2,1)S(1)}, bf16[96,2]{0,1:T(2,128)(2,1)}, u32[]{:S(2)}) copy-start(bf16[96,2]{0,1:T(2,128)(2,1)} %param.13) | copy-start | bytes 1156
  7.2 47.0 %copy-start.13 = (s32[96]{0:T(128)S(1)}, s32[96]{0:T(128)}, u32[]{:S(2)}) copy-start(s32[96]{0:T(128)} %param.14) | copy-start | bytes 1156
  7.2 72.4 %all-gather.5.cloned.1.call-start = ((), (), s32[]{:S(2)}) async-start(), calls=%async_computation.6 | async-start | bytes 1769472 | tf_op jit(solution)/shard_map/all_gather | solution.py:75
  8.1 71.5 %copy-start.2 = (bf16[1,3072,128]{2,1,0:T(8,128)(2,1)S(1)}, bf16[1,3072,128]{2,1,0:T(8,128)(2,1)}, u32[]{:S(2)}) copy-start(bf16[1,3072,128]{2,1,0:T(8,128)(2,1)} %param.15) | copy-start | bytes 2359300
  36.6 88.4 %all-gather.3.cloned.1.call-start = ((), (), s32[]{:S(2)}) async-start(), calls=%async_computation.5 | async-start | bytes 1769472 | tf_op jit(solution)/shard_map/all_gather | solution.py:76
  53.8 416.4 %reduce-scatter.4.cloned.1.call-start = ((), (), s32[]{:S(2)}) async-start(), calls=%async_computation.8 | async-start | bytes 3170304
  79.6 2.1 copy-start.4
  81.7 43.3 %copy-start.5 = (bf16[1,128,3072]{2,1,0:T(8,128)(2,1)S(1)}, bf16[1,128,3072]{2,1,0:T(8,128)(2,1)}, u32[]{:S(2)}) copy-start(bf16[1,128,3072]{2,1,0:T(8,128)(2,1)} %param.19) | copy-start | bytes 2359300
  83.0 44.2 %copy-start.11 = (bf16[1,128,128]{2,1,0:T(8,128)(2,1)S(1)}, bf16[1,128,128]{2,1,0:T(8,128)(2,1)}, u32[]{:S(2)}) copy-start(bf16[1,128,128]{2,1,0:T(8,128)(2,1)} %param.18) | copy-start | bytes 98308
  83.0 44.3 %copy-start.6 = (bf16[1,128,3072]{2,1,0:T(8,128)(2,1)S(1)}, bf16[1,128,3072]{2,1,0:T(8,128)(2,1)}, u32[]{:S(2)}) copy-start(bf16[1,128,3072]{2,1,0:T(8,128)(2,1)} %param.17) | copy-start | bytes 2359300
  125.0 2.3 copy-start.1
  127.1 0.8 copy-start.7
  127.1 0.9 copy-start.10
  134.4 0.8 copy-start.9
  134.4 345.9 %copy-start.8 = (bf16[256,128]{1,0:T(8,128)(2,1)S(1)}, bf16[256,128]{1,0:T(8,128)(2,1)}, u32[]{:S(2)}) copy-start(bf16[256,128]{1,0:T(8,128)(2,1)} %copy-done.7) | copy-start | bytes 196612
  134.4 2344.1 %copy-start.3 = (bf16[8,32,384]{2,1,0:T(8,128)(2,1)S(1)}, bf16[8,32,384]{2,1,0:T(8,128)(2,1)}, u32[]{:S(2)}) copy-start(bf16[8,32,384]{2,1,0:T(8,128)(2,1)} %all_to_all.21) | copy-start | bytes 589828
  134.5 2344.0 %all-reduce.3.cloned.1.call-start = ((), (), s32[]{:S(2)}) async-start(), calls=%async_computation.7 | async-start | bytes 262144 | tf_op jit(solution)/shard_map/psum | solution.py:97
  471.9 2008.4 %all-to-all-start.3 = ((f32[8,1,768]{2,1,0:T(1,128)}), f32[8,1,768]{2,1,0:T(1,128)S(1)}, u32[]{:S(2)}, u32[]{:S(2)}) async-start(f32[8,1,768]{2,1,0:T(1,128)} %reshape.111), calls=%async_computation.3 | async-start | bytes 49152 | tf_op jit(solution)/shard_map/all_to_all | solution.py:132
Sparse Core Ops, SparseCore 0:
  36.7 42.8 all-gather.4
  82.3 42.6 all-gather.2
  134.6 335.6 reduce-scatter.3
  474.2 2004.2 all-reduce.2
where the time goes:
time: 2490 us
  waiting for transfers between devices  2380 us (96%)
  blocking collectives  56.7 us (2%)
    psum x1, waiting for transfers between devices, on_device(): low_in = lax.psum(low_part, ('dp', 'tensor'))  2000 us
    unnamed x5, waiting for transfers between devices  334 us
  transfers between devices with their start and end apart: 5, of which 4 were waited for; matrix products, arithmetic and copies ran while one was open for 0% of the time, Pallas kernels for 0%

commit v1 on v0

v1 whole, which is shorter than its diff:
```python
import jax
import jax.numpy as jnp
from jax import lax
from jax.sharding import Mesh, PartitionSpec as P

TEN = 8
RANK = 16
CAP = 32
SCALE = 2.0
BF = jnp.bfloat16
F32 = jnp.float32


def dot(a, b, ca, cb, precision=None):
    return lax.dot_general(
        a, b, (((ca,), (cb,)), ((), ())), precision=precision, preferred_element_type=F32
    )


def hot(index, size):
    return lax.broadcasted_iota(jnp.int32, (index.shape[0], size), 1) == index


def on_device(
    tokens,
    cotangent,
    expert_ids,
    gate_probs,
    tenant_ids,
    w_gate,
    w_up,
    w_down,
    adapter_in,
    adapter_out,
):
    nz, nx, ne, ny, nc = (lax.axis_size(a) for a in ("zh", "x", "e", "y", "c"))
    nxy = nx * ny
    group, width = tokens.shape
    slots = ne * CAP
    part = CAP // nx
    me_x, me_e, me_y, me_c = (lax.axis_index(a) for a in ("x", "e", "y", "c"))
    swap = [(0, 1), (1, 0)]
    gate_mat, up_mat, down_mat = w_gate[0], w_up[0], w_down[0]
    first, second = adapter_in[0], adapter_out[0]
    features = gate_mat.shape[0]
    piece = features // (nz * nxy * nc)

    named = [hot(expert_ids[:, j : j + 1], ne) for j in range(2)]
    either = (named[0] | named[1]).astype(BF)
    before = (
        lax.broadcasted_iota(jnp.int32, (group, group), 1)
        < lax.broadcasted_iota(jnp.int32, (group, group), 0)
    ).astype(BF)
    earlier = dot(before, either, 1, 0)
    slot = [
        jnp.sum(jnp.where(n, earlier, 0.0), axis=1, keepdims=True).astype(jnp.int32) for n in named
    ]
    tenant = tenant_ids[:, None]

    pick, marks, combine = None, None, None
    for j in range(2):
        expert = expert_ids[:, j : j + 1]
        quarter, rest = slot[j] // part, slot[j] % part
        here = hot(expert * part + rest, ne * part)
        mine = (here & (quarter == me_x)).astype(BF)
        weighted = here.astype(BF) * gate_probs[:, j : j + 1]
        mark = dot(weighted, hot(quarter * TEN + tenant, nx * TEN).astype(BF), 0, 0)
        back = hot(expert * CAP + slot[j], slots).astype(F32)
        pick = mine if pick is None else pick + mine
        marks = mark if marks is None else marks + mark
        combine = back if combine is None else combine + back
    rows = dot(pick, jnp.concatenate([tokens, cotangent], axis=1), 0, 0).astype(BF)
    pad = -(nx * TEN) % 128
    send = jnp.concatenate([rows, jnp.pad(marks.astype(BF), ((0, 0), (0, pad)))], axis=1)
    held = lax.all_to_all(
        send.reshape(ne, part, -1), "e", split_axis=0, concat_axis=0, tiled=True
    ).reshape(ne * part, -1)

    quarter_rows = ne * part
    block = held[:, : 2 * width]
    own = lax.all_to_all(
        jnp.broadcast_to(block[None], (nxy, quarter_rows, 2 * width)),
        ("y", "x"),
        split_axis=0,
        concat_axis=0,
        tiled=True,
    )
    other = lax.ppermute(own, "c", swap)
    low_core, high_core = jnp.where(me_c == 0, own, other), jnp.where(me_c == 0, other, own)
    both = jnp.stack([low_core, high_core]).reshape(nc, ny, nx, quarter_rows, 2, width)
    both = both.transpose(4, 2, 3, 1, 0, 5).reshape(2, slots, features)
    x_rows, y_rows = both[0], both[1]
    row_marks = held[:, 2 * width : 2 * width + nx * TEN].reshape(quarter_rows, nx, TEN)
    row_marks = row_marks.transpose(1, 0, 2).reshape(slots, TEN)
    column_of = lax.broadcasted_iota(jnp.int32, (TEN, TEN * RANK), 1) // RANK
    spread = (column_of == lax.broadcasted_iota(jnp.int32, (TEN, TEN * RANK), 0)).astype(BF)
    flags = dot(row_marks, spread, 1, 0)
    row_weight = jnp.sum(row_marks.astype(F32), axis=1, keepdims=True)

    gate_acc = dot(x_rows, gate_mat, 1, 0)
    up_acc = dot(x_rows, up_mat, 1, 0)
    back_acc = dot(y_rows, down_mat, 1, 1)
    low_back = dot(y_rows, second, 1, 1)
    sig = jax.nn.sigmoid(gate_acc)
    silu = gate_acc * sig
    hidden = (silu * up_acc).astype(BF)
    low_part = dot(hidden, first, 1, 0)
    down_coef = (SCALE * flags * low_back).astype(BF)
    hidden_grad = row_weight * back_acc + dot(down_coef, first, 1, 1)
    slope = sig * (1.0 + gate_acc * (1.0 - sig))
    gate_grad = (hidden_grad * up_acc * slope).astype(BF)
    up_grad = (hidden_grad * silu).astype(BF)
    grad_a = dot(hidden, down_coef, 0, 0)

    rank_of = lax.broadcasted_iota(jnp.int32, (TEN * RANK, RANK), 0) % RANK
    fold = (rank_of == lax.broadcasted_iota(jnp.int32, (TEN * RANK, RANK), 1)).astype(BF)
    kept = jnp.where(flags != 0.0, low_part, 0.0).astype(BF)
    low_rows = dot(fold, kept, 0, 1).astype(BF)
    term = dot(gate_mat, gate_grad, 1, 1) + dot(up_mat, up_grad, 1, 1)
    term = term.astype(BF).reshape(nz, nxy, nc, piece, slots).transpose(2, 1, 0, 3, 4)
    term = term.reshape(nc, nxy, nz * piece, slots)
    extra = jnp.pad(low_rows[:, None, :], ((0, 0), (0, 7), (0, 0)))
    term = jnp.concatenate([term, jnp.broadcast_to(extra[None], (nc,) + extra.shape)], axis=2)
    keep = lax.dynamic_index_in_dim(term, me_c, 0, keepdims=False)
    give = lax.dynamic_index_in_dim(term, 1 - me_c, 0, keepdims=False)
    pair = (keep.astype(F32) + lax.ppermute(give, "c", swap).astype(F32)).astype(BF)
    plane = lax.all_to_all(pair, ("x", "y"), split_axis=0, concat_axis=0, tiled=True)
    plane = jnp.sum(plane.astype(F32), axis=0).astype(BF)

    feats = plane[: nz * piece].reshape(nz, piece, nx, ne, part).transpose(0, 3, 1, 2, 4)
    lanes = 128
    feats = feats.reshape(nz * ne, piece * CAP // lanes, lanes)
    low_line = plane[nz * piece].reshape(1, slots // lanes, lanes)
    outgoing = jnp.concatenate(
        [feats, jnp.broadcast_to(low_line, (nz * ne, slots // lanes, lanes))], axis=1
    )
    came = lax.all_to_all(outgoing, ("zh", "e"), split_axis=0, concat_axis=0, tiled=True)
    came = came.reshape(nz, ne, -1, lanes)
    n_feat = piece * CAP // lanes
    total = jnp.sum(came.astype(F32), axis=0)
    returned = total[:, :n_feat].reshape(ne, piece, CAP).transpose(1, 0, 2).reshape(piece, slots)
    input_grad = dot(combine, returned, 1, 1, lax.Precision.HIGHEST).astype(BF)

    low_mine = lax.dynamic_index_in_dim(total, me_e, 0, keepdims=False)[n_feat:]
    low_all = lax.all_gather(low_mine, ("x", "y"), axis=0, tiled=False).reshape(RANK, slots)
    tiled = jnp.tile(low_all, (TEN, 1))
    up_coef = (SCALE * flags * tiled.T).astype(BF)
    local = lax.dynamic_index_in_dim(
        own.reshape(ny, nx * quarter_rows, 2 * width), me_y, 0, keepdims=False
    )[:, width:]
    grad_b = dot(up_coef, local, 0, 0)
    return input_grad, grad_a[None], grad_b[None]


def solution(mesh):
    tensor, dp, expert = mesh.shape["tensor"], mesh.shape["dp"], mesh.shape["expert"]
    fine = Mesh(
        mesh.devices.reshape(dp // 4, 4, expert, tensor // 2, 2), ("zh", "x", "e", "y", "c")
    )
    units, cols = ("zh", "x", "y", "c"), ("y", "c")
    return jax.shard_map(
        on_device,
        mesh=fine,
        in_specs=(
            P("e", cols),
            P("e", cols),
            P("e", None),
            P("e", None),
            P("e"),
            P("e", None, units),
            P("e", None, units),
            P("e", units, None),
            P("e", units, None),
            P("e", None, None),
        ),
        out_specs=(P("e", units), P("e", units, None), P("e", None, cols)),
        check_vma=False,
    )
```

time: 2490 us -> 213 us (0.09)
  waiting for transfers between devices: 2380 us -> 26.5 us
  blocking collectives: 56.7 us -> 90 us
  local copies, waits for them, and re-layouts: 8.86 us -> 39 us
    psum x1 -> x0, waiting for transfers between devices: 2000 us -> none  [on_device(): low_in = lax.psum(low_part, ('dp', 'tensor'))]
    unnamed x5 -> x0, waiting for transfers between devices: 334 us -> none
    all_gather x2 -> x0, waiting for transfers between devices: 51.7 us -> none  [the longest x1 42 us: on_device(): grad_piece = lax.all_gather(recv_grads, 'tensor', axis=2, tiled=True)]
  transfers between devices with their start and end apart: 5 -> 3, of which waited for: 4 -> 3; matrix products, arithmetic and copies ran while one was open for 0% -> 1% of each run, Pallas kernels for 0% -> 0%
where the time goes in v1:
time: 213 us; the launch traced here: 212 us
  blocking collectives  90 us (42%)
  local copies, waits for them, and re-layouts  39 us (18%)
  starting transfers between devices  26.8 us (13%)
  waiting for transfers between devices  26.5 us (12%)
  other arithmetic  15 us (7%)
  matrix products  13.8 us (6%)
    all_to_all x1, blocking collectives, on_device(): lax.all_to_all(jnp.broadcast_to(block[None], (nxy, quarter_rows, 2 * widt...  25.5 us
    all_to_all x1, blocking collectives, on_device(): lax.all_to_all(send.reshape(ne, part, -1), 'e', split_axis=0, concat_axis...  24.7 us
    all_to_all x1, starting transfers between devices, on_device(): lax.all_to_all(outgoing, ('zh', 'e'), split_axis=0, concat_axis=0, tiled=...  22.9 us
    all_gather x1, blocking collectives, on_device(): lax.all_gather(low_mine, ('x', 'y'), axis=0, tiled=False)  21.8 us
    all_to_all x1, waiting for transfers between devices, on_device(): lax.all_to_all(outgoing, ('zh', 'e'), split_axis=0, concat_axis=0, tiled=...  21.5 us
    all_to_all x1, blocking collectives, on_device(): lax.all_to_all(pair, ('x', 'y'), split_axis=0, concat_axis=0, tiled=True)  18 us
    slice x3, local copies, waits for them, and re-layouts, on_device(): x_rows, y_rows = (both[0], both[1])  14.6 us
    dot_general x16, matrix products, dot(): lax.dot_general(a, b, (((ca,), (cb,)), ((), ())), precision=precision, pr...  13.8 us
  transfers between devices with their start and end apart: 3, of which 3 were waited for; matrix products, arithmetic and copies ran while one was open for 1% of the time, Pallas kernels for 0%

profile of v1, /device:TPU:32, one launch (start us, length us, event | category | flops | bytes accessed | tf_op | source)
XLA Modules:
  0.0 211.9 jit_solution(5694131551077057588)
XLA Ops:
  0.7 0.7 slice_bitcast_fusion
  1.4 0.8 slice_bitcast_fusion.3
  2.3 1.3 fusion.90
  3.6 0.7 multiply_add_fusion
  4.3 0.3 fusion.49
  4.6 0.3 fusion.7
  4.9 1.2 convolution_convert_fusion
  6.2 24.7 %all_to_all.20 = bf16[8,8,896]{2,1,0:T(8,128)(2,1)S(1)} all-to-all(bf16[8,8,896]{2,1,0:T(8,128)(2,1)S(1)} %fusion.32), channel_id=1, replica_groups=mesh['zh'=4,'x'=4,'e'=8,'y'=4,'c'=2] {'e'}, dimensions={0} | all-to-all | bytes 229376 | tf_op jit(solution)/shard_map/all_to_all | solution.py:75
  31.0 25.5 %all_to_all.21 = bf16[16,64,768]{2,1,0:T(8,128)(2,1)S(1)} all-to-all(bf16[16,64,768]{2,1,0:T(8,128)(2,1)S(1)} %broadcast_in_dim.40), channel_id=1, replica_groups=mesh['zh'=4,'x'=4,'e'=8,'y'=4,'c'=2] {'y','x'}, dimensions={0} | all-to-all | bytes 3145728 | tf_op jit(solution)/shard_map/all_to_all | solution.py:81
  56.5 1.9 collective-permute-start
  58.6 0.7 mul.93
  59.4 0.2 fusion.79
  59.6 2.4 %collective-permute-done = bf16[16,64,768]{2,1,0:T(8,128)(2,1)} collective-permute-done((bf16[16,64,768]{2,1,0:T(8,128)(2,1)S(1)}, bf16[16,64,768]{2,1,0:T(8,128)(2,1)}, u32[]{:S(2)}, u32[]{:S(2)}) %collective-permute-start) | collective-permute-done | bytes 1572896 | tf_op jit(solution)/shard_map/ppermute | solution.py:88
  62.0 3.3 %broadcast_select_fusion.1 = (bf16[16,64,768]{2,1,0:T(8,128)(2,1)}, bf16[16,64,768]{2,1,0:T(8,128)(2,1)}) fusion(bf16[16,64,768]{2,1,0:T(8,128)(2,1)S(1)} %all_to_all.21, bf16[16,64,768]{2,1,0:T(8,128)(2,1)} %collective-permute-done, pred[]{:T(512)S(6)} %eq.136), kind=kLoop, calls=%fused_computation.9 | loop fusion | flops 1572864 | bytes 6291457 | tf_op jit(solution)/shard_map/jit(_where)/select_n | solution.py:89
  65.2 4.5 %stack.9 = bf16[1,4,4,64,2,384]{5,4,3,2,1,0:T(2,128)(2,1)} reshape(bf16[16,64,768]{2,1,0:T(8,128)(2,1)} %get-tuple-element.11) | data formatting | bytes 3145728 | tf_op jit(solution)/shard_map/stack | solution.py:90
  69.7 1.3 stack.10
  71.0 6.6 %maximum_bitcast_fusion = bf16[2,4,64,4,2,384]{5,0,2,1,3,4:T(2,128)(2,1)S(1)} fusion(bf16[1,4,4,64,2,384]{5,4,3,2,1,0:T(2,128)(2,1)} %stack.10, bf16[1,4,4,64,2,384]{5,4,3,2,1,0:T(2,128)(2,1)} %stack.9), kind=kLoop, calls=%fused_computation.3 | loop fusion | flops 1572864 | bytes 6291456 | tf_op jit(solution)/shard_map/transpose | solution.py:91
  77.6 5.5 %fusion.100 = (bf16[1,4,64,4,2,384]{5,0,2,1,3,4:T(2,128)(2,1)S(1)}, bf16[1,4,64,4,2,384]{5,0,2,1,3,4:T(2,128)(2,1)}) fusion(bf16[2,4,64,4,2,384]{5,0,2,1,3,4:T(2,128)(2,1)S(1)} %maximum_bitcast_fusion), kind=kLoop, calls=%fused_computation.165 | loop fusion | bytes 6291456 | tf_op jit(solution)/shard_map/slice | solution.py:92
  83.2 3.6 %copy.54 = bf16[1,4,64,4,2,384]{5,4,3,2,1,0:T(2,128)(2,1)} copy(bf16[1,4,64,4,2,384]{5,0,2,1,3,4:T(2,128)(2,1)S(1)} %get-tuple-element.9) | data formatting | bytes 3145728 | tf_op jit(solution)/shard_map/slice | solution.py:92
  86.8 4.1 %squeeze.32 = bf16[256,3072]{1,0:T(8,128)(2,1)S(1)} reshape(bf16[1,4,64,4,2,384]{5,4,3,2,1,0:T(2,128)(2,1)} %copy.54) | data formatting | bytes 3145728 | tf_op jit(solution)/shard_map/squeeze | solution.py:92
  90.8 5.5 %copy.56 = bf16[1,4,64,4,2,384]{5,4,3,2,1,0:T(2,128)(2,1)} copy(bf16[1,4,64,4,2,384]{5,0,2,1,3,4:T(2,128)(2,1)} %get-tuple-element.10) | data formatting | bytes 3145728 | tf_op jit(solution)/shard_map/slice | solution.py:92
  96.3 4.9 %squeeze.36 = bf16[256,3072]{1,0:T(8,128)(2,1)} reshape(bf16[1,4,64,4,2,384]{5,4,3,2,1,0:T(2,128)(2,1)} %copy.56) | data formatting | bytes 3145728 | tf_op jit(solution)/shard_map/squeeze | solution.py:92
  101.2 1.9 fusion.4
  103.0 0.8 fusion.54
  103.9 0.6 fusion.16
  104.4 1.2 multiply_convert_fusion
  105.6 1.7 fusion.9
  107.3 0.7 copy.65
  108.1 1.8 fusion.3
  109.9 0.6 fusion.14
  110.4 0.6 fusion.1
  111.0 1.6 copy.57
  112.6 1.6 copy.58
  114.3 1.0 fusion.11
  115.2 2.0 collective-permute-start.1
  117.3 2.6 %collective-permute-done.1 = bf16[16,104,256]{2,1,0:T(8,128)(2,1)} collective-permute-done((bf16[16,104,256]{2,1,0:T(8,128)(2,1)}, bf16[16,104,256]{2,1,0:T(8,128)(2,1)}, u32[]{:S(2)}, u32[]{:S(2)}) %collective-permute-start.1) | collective-permute-done | bytes 852000 | tf_op jit(solution)/shard_map/ppermute | solution.py:126
  119.8 1.4 fusion.2
  121.2 18.0 %all_to_all.22 = bf16[16,104,256]{2,1,0:T(8,128)(2,1)S(1)} all-to-all(bf16[16,104,256]{2,1,0:T(8,128)(2,1)S(1)} %fusion.2), channel_id=1, replica_groups=mesh['zh'=4,'x'=4,'e'=8,'y'=4,'c'=2] {'x','y'}, dimensions={0} | all-to-all | bytes 1703936 | tf_op jit(solution)/shard_map/all_to_all | solution.py:127
  139.6 0.6 copy.61
  140.2 0.8 reshape.257
  141.1 0.7 pad_maximum_fusion
  141.7 22.9 %all-to-all-start.3 = ((bf16[32,8,128]{2,1,0:T(8,128)(2,1)}), bf16[32,8,128]{2,1,0:T(8,128)(2,1)S(1)}, u32[]{:S(2)}, u32[]{:S(2)}) async-start(bf16[32,8,128]{2,1,0:T(8,128)(2,1)} %pad_maximum_fusion), calls=%async_computation.3 | async-start | bytes 131072 | tf_op jit(solution)/shard_map/all_to_all | solution.py:137
  164.6 1.0 dynamic-slice_bitcast_fusion
  165.6 0.8 convolution_bitcast_fusion.1
  166.5 21.5 %all-to-all-done.3 = bf16[32,8,128]{2,1,0:T(8,128)(2,1)S(1)} async-done(((bf16[32,8,128]{2,1,0:T(8,128)(2,1)}), bf16[32,8,128]{2,1,0:T(8,128)(2,1)S(1)}, u32[]{:S(2)}, u32[]{:S(2)}) %all-to-all-start.3) | async-done | bytes 65568 | tf_op jit(solution)/shard_map/all_to_all | solution.py:137
  188.1 21.8 %all_gather.4 = f32[16,2,128]{2,1,0:T(2,128)S(1)} all-gather(f32[1,2,128]{2,1,0:T(2,128)S(1)} %slice.55), channel_id=1, replica_groups=mesh['zh'=4,'x'=4,'e'=8,'y'=4,'c'=2] {'x','y'}, dimensions={0}, use_global_device_ids=true | all-gather | bytes 17408 | tf_op jit(solution)/shard_map/all_gather | solution.py:145
  210.2 0.9 convolution_bitcast_fusion
  211.1 0.9 convolution_convert_fusion.1
  (50 shorter events, 1.5 us)
Async XLA Ops:
  0.6 103.8 %copy-start = (bf16[1,3072,128]{2,1,0:T(8,128)(2,1)S(1)}, bf16[1,3072,128]{2,1,0:T(8,128)(2,1)}, u32[]{:S(2)}) copy-start(bf16[1,3072,128]{2,1,0:T(8,128)(2,1)} %param.16) | copy-start | bytes 2359300
  56.5 8.7 %copy-start.1 = (bf16[16,64,768]{2,1,0:T(8,128)(2,1)}, bf16[16,64,768]{2,1,0:T(8,128)(2,1)S(1)}, u32[]{:S(2)}) copy-start(bf16[16,64,768]{2,1,0:T(8,128)(2,1)S(1)} %all_to_all.21) | copy-start | bytes 4718596
  56.5 5.4 %collective-permute-start = (bf16[16,64,768]{2,1,0:T(8,128)(2,1)S(1)}, bf16[16,64,768]{2,1,0:T(8,128)(2,1)}, u32[]{:S(2)}, u32[]{:S(2)}) collective-permute-start(bf16[16,64,768]{2,1,0:T(8,128)(2,1)S(1)} %all_to_all.21), channel_id=1, source_target_pairs={{0,1},{1,0},{2,3},{3,2},{4,5},{5,4},{6,7},{7,6},{8,9},{9,8},{10,11... | collective-permute-start | bytes 4718600 | tf_op jit(solution)/shard_map/ppermute | solution.py:88
  65.2 4.5 %copy-start.3 = (bf16[16,64,768]{2,1,0:T(8,128)(2,1)S(1)}, bf16[16,64,768]{2,1,0:T(8,128)(2,1)}, u32[]{:S(2)}) copy-start(bf16[16,64,768]{2,1,0:T(8,128)(2,1)} %get-tuple-element.12) | copy-start | bytes 4718596
  101.2 1.9 copy-start.6
  101.2 2.7 %copy-start.2 = (bf16[256,3072]{1,0:T(8,128)(2,1)S(1)}, bf16[256,3072]{1,0:T(8,128)(2,1)}, u32[]{:S(2)}) copy-start(bf16[256,3072]{1,0:T(8,128)(2,1)} %squeeze.36) | copy-start | bytes 4718596
  101.2 2.7 %copy-start.4 = (bf16[1,3072,128]{2,1,0:T(8,128)(2,1)S(1)}, bf16[1,3072,128]{2,1,0:T(8,128)(2,1)}, u32[]{:S(2)}) copy-start(bf16[1,3072,128]{2,1,0:T(8,128)(2,1)} %param.15) | copy-start | bytes 2359300
  107.3 2.5 %copy-start.5 = (f32[256,128]{1,0:T(8,128)S(1)}, f32[256,128]{1,0:T(8,128)}, u32[]{:S(2)}) copy-start(f32[256,128]{1,0:T(8,128)} %get-tuple-element.26) | copy-start | bytes 393220
  115.2 4.6 %collective-permute-start.1 = (bf16[16,104,256]{2,1,0:T(8,128)(2,1)}, bf16[16,104,256]{2,1,0:T(8,128)(2,1)}, u32[]{:S(2)}, u32[]{:S(2)}) collective-permute-start(bf16[16,104,256]{2,1,0:T(8,128)(2,1)} %fusion.11), channel_id=1, source_target_pairs={{0,1},{1,0},{2,3},{3,2},{4,5},{5,4},{6,7},{7,6},{8,9},{9,8},{10,11... | collective-permute-start | bytes 2555912 | tf_op jit(solution)/shard_map/ppermute | solution.py:126
  141.0 70.0 %copy-start.7 = (s32[96]{0:T(128)S(1)}, s32[96]{0:T(128)}, u32[]{:S(2)}) copy-start(s32[96]{0:T(128)} %get-tuple-element.13) | copy-start | bytes 1156
  141.0 70.0 %copy-start.8 = (s32[96]{0:T(128)S(1)}, s32[96]{0:T(128)}, u32[]{:S(2)}) copy-start(s32[96]{0:T(128)} %get-tuple-element.18) | copy-start | bytes 1156
  141.7 46.3 %all-to-all-start.3 = ((bf16[32,8,128]{2,1,0:T(8,128)(2,1)}), bf16[32,8,128]{2,1,0:T(8,128)(2,1)S(1)}, u32[]{:S(2)}, u32[]{:S(2)}) async-start(bf16[32,8,128]{2,1,0:T(8,128)(2,1)} %pad_maximum_fusion), calls=%async_computation.3 | async-start | bytes 131072 | tf_op jit(solution)/shard_map/all_to_all | solution.py:137

commit v2 on v1

--- a/solution.py
+++ b/solution.py
@@ -1,6 +1,10 @@
+import functools
+
 import jax
 import jax.numpy as jnp
 from jax import lax
+from jax.experimental import pallas as pl
+from jax.experimental.pallas import tpu as pltpu
 from jax.sharding import Mesh, PartitionSpec as P
 
 TEN = 8
@@ -19,6 +23,78 @@
 
 def hot(index, size):
     return lax.broadcasted_iota(jnp.int32, (index.shape[0], size), 1) == index
+
+
+def expert_kernel(
+    sizes, core, own, other, held_marks, gate_mat, up_mat, down_mat, first, second,
+    keep, give, hidden_out, down_out, flags_out, terms,
+):
+    nz, nx, ny, nc = sizes
+    nxy = nx * ny
+    mine = core[0]
+    quarter_rows, width = own.shape[1], own.shape[2] // 2
+    slots = nx * quarter_rows
+    features = gate_mat.shape[0]
+    part, piece = features // nz, features // (nz * nxy * nc)
+    low_width = first.shape[1]
+
+    forward, backward = None, None
+    for y in range(ny):
+        for ref, at_core in ((own, mine), (other, 1 - mine)):
+            at = pl.multiple_of((y * nc + at_core) * width, 128)
+            both = ref[y * nx : (y + 1) * nx].reshape(slots, 2 * width)
+            mats = jnp.concatenate([gate_mat[pl.ds(at, width), :], up_mat[pl.ds(at, width), :]], 1)
+            ahead = dot(both[:, :width], mats, 1, 0)
+            mats = jnp.concatenate([down_mat[:, pl.ds(at, width)], second[:, pl.ds(at, width)]], 0)
+            behind = dot(both[:, width:], mats, 1, 1)
+            forward = ahead if forward is None else forward + ahead
+            backward = behind if backward is None else backward + behind
+    units = gate_mat.shape[1]
+    gate_acc, up_acc = forward[:, :units], forward[:, units:]
+    back_acc, low_back = backward[:, :units], backward[:, units:]
+
+    mark_rows = held_marks[...]
+    lane = lax.broadcasted_iota(jnp.int32, (mark_rows.shape[1], low_width), 0)
+    tenant_of = lax.broadcasted_iota(jnp.int32, (mark_rows.shape[1], low_width), 1) // RANK
+    flags, weight = [], []
+    for x in range(nx):
+        flags.append(dot(mark_rows, (lane == x * TEN + tenant_of).astype(BF), 1, 0))
+        inside = (lane >= x * TEN) & (lane < (x + 1) * TEN)
+        weight.append(dot(mark_rows, inside.astype(BF), 1, 0))
+    flags, weight = jnp.concatenate(flags, 0), jnp.concatenate(weight, 0)[:, :1]
+
+    sig = jax.nn.sigmoid(gate_acc)
+    silu = gate_acc * sig
+    hidden = (silu * up_acc).astype(BF)
+    low_part = dot(hidden, first[...], 1, 0)
+    down_coef = (SCALE * flags * low_back).astype(BF)
+    hidden_grad = weight * back_acc + dot(down_coef, first[...], 1, 1)
+    slope = sig * (1.0 + gate_acc * (1.0 - sig))
+    gate_grad = (hidden_grad * up_acc * slope).astype(BF)
+    up_grad = (hidden_grad * silu).astype(BF)
+    hidden_out[...] = hidden
+    down_out[...] = down_coef
+    flags_out[...] = flags
+
+    grads = jnp.concatenate([gate_grad, up_grad], 1)
+    for z in range(nz):
+        at = slice(z * part, (z + 1) * part)
+        mats = jnp.concatenate([gate_mat[at, :], up_mat[at, :]], 1)
+        terms[at, :] = dot(mats, grads, 1, 1)
+
+    rank_of = lax.broadcasted_iota(jnp.int32, (RANK, low_width), 1) % RANK
+    fold = (rank_of == lax.broadcasted_iota(jnp.int32, (RANK, low_width), 0)).astype(BF)
+    kept = jnp.where(flags != 0.0, low_part, 0.0).astype(BF)
+    low_rows = dot(fold, kept, 1, 1)
+    under = lax.broadcasted_iota(jnp.int32, (16, slots), 0) == 0
+    for p in range(nxy):
+        for out, at_core in ((keep, mine), (give, 1 - mine)):
+            chunks = [
+                terms[pl.ds(pl.multiple_of(z * part + (p * nc + at_core) * piece, 8), piece), :]
+                for z in range(nz)
+            ]
+            chunks.append(jnp.where(under, low_rows[p : p + 1, :], 0.0))
+            out[p] = jnp.concatenate(chunks, 0).astype(out.dtype)
 
 
 def on_device(
@@ -86,44 +162,39 @@
         tiled=True,
     )
     other = lax.ppermute(own, "c", swap)
-    low_core, high_core = jnp.where(me_c == 0, own, other), jnp.where(me_c == 0, other, own)
-    both = jnp.stack([low_core, high_core]).reshape(nc, ny, nx, quarter_rows, 2, width)
-    both = both.transpose(4, 2, 3, 1, 0, 5).reshape(2, slots, features)
-    x_rows, y_rows = both[0], both[1]
-    row_marks = held[:, 2 * width : 2 * width + nx * TEN].reshape(quarter_rows, nx, TEN)
-    row_marks = row_marks.transpose(1, 0, 2).reshape(slots, TEN)
-    column_of = lax.broadcasted_iota(jnp.int32, (TEN, TEN * RANK), 1) // RANK
-    spread = (column_of == lax.broadcasted_iota(jnp.int32, (TEN, TEN * RANK), 0)).astype(BF)
-    flags = dot(row_marks, spread, 1, 0)
-    row_weight = jnp.sum(row_marks.astype(F32), axis=1, keepdims=True)
-
-    gate_acc = dot(x_rows, gate_mat, 1, 0)
-    up_acc = dot(x_rows, up_mat, 1, 0)
-    back_acc = dot(y_rows, down_mat, 1, 1)
-    low_back = dot(y_rows, second, 1, 1)
-    sig = jax.nn.sigmoid(gate_acc)
-    silu = gate_acc * sig
-    hidden = (silu * up_acc).astype(BF)
-    low_part = dot(hidden, first, 1, 0)
-    down_coef = (SCALE * flags * low_back).astype(BF)
-    hidden_grad = row_weight * back_acc + dot(down_coef, first, 1, 1)
-    slope = sig * (1.0 + gate_acc * (1.0 - sig))
-    gate_grad = (hidden_grad * up_acc * slope).astype(BF)
-    up_grad = (hidden_grad * silu).astype(BF)
+    units, low_width = gate_mat.shape[1], first.shape[1]
+    tall = nz * piece + 16
+    in_vmem = pl.BlockSpec(memory_space=pltpu.VMEM)
+    keep, give, hidden, down_coef, flags = pl.pallas_call(
+        functools.partial(expert_kernel, (nz, nx, ny, nc)),
+        out_shape=(
+            jax.ShapeDtypeStruct((nxy, tall, slots), F32),
+            jax.ShapeDtypeStruct((nxy, tall, slots), BF),
+            jax.ShapeDtypeStruct((slots, units), BF),
+            jax.ShapeDtypeStruct((slots, low_width), BF),
+            jax.ShapeDtypeStruct((slots, low_width), F32),
+        ),
+        in_specs=[pl.BlockSpec(memory_space=pltpu.SMEM)] + [in_vmem] * 8,
+        out_specs=(in_vmem,) * 5,
+        scratch_shapes=[pltpu.VMEM((features, slots), F32)],
+        compiler_params=pltpu.CompilerParams(vmem_limit_bytes=40 << 20),
+        cost_estimate=pl.CostEstimate(
+            flops=10 * slots * features * units, bytes_accessed=9 << 20, transcendentals=slots * units
+        ),
+    )(
+        me_c.reshape(1).astype(jnp.int32),
+        own,
+        other,
+        held[:, 2 * width :],
+        gate_mat,
+        up_mat,
+        down_mat,
+        first,
+        second,
+    )
     grad_a = dot(hidden, down_coef, 0, 0)
-
-    rank_of = lax.broadcasted_iota(jnp.int32, (TEN * RANK, RANK), 0) % RANK
-    fold = (rank_of == lax.broadcasted_iota(jnp.int32, (TEN * RANK, RANK), 1)).astype(BF)
-    kept = jnp.where(flags != 0.0, low_part, 0.0).astype(BF)
-    low_rows = dot(fold, kept, 0, 1).astype(BF)
-    term = dot(gate_mat, gate_grad, 1, 1) + dot(up_mat, up_grad, 1, 1)
-    term = term.astype(BF).reshape(nz, nxy, nc, piece, slots).transpose(2, 1, 0, 3, 4)
-    term = term.reshape(nc, nxy, nz * piece, slots)
-    extra = jnp.pad(low_rows[:, None, :], ((0, 0), (0, 7), (0, 0)))
-    term = jnp.concatenate([term, jnp.broadcast_to(extra[None], (nc,) + extra.shape)], axis=2)
-    keep = lax.dynamic_index_in_dim(term, me_c, 0, keepdims=False)
-    give = lax.dynamic_index_in_dim(term, 1 - me_c, 0, keepdims=False)
-    pair = (keep.astype(F32) + lax.ppermute(give, "c", swap).astype(F32)).astype(BF)
+    pair = keep + lax.ppermute(give, "c", swap).astype(F32)
+    pair = pair[:, : nz * piece + 8].astype(BF)
     plane = lax.all_to_all(pair, ("x", "y"), split_axis=0, concat_axis=0, tiled=True)
     plane = jnp.sum(plane.astype(F32), axis=0).astype(BF)
 
@@ -142,7 +213,13 @@
     input_grad = dot(combine, returned, 1, 1, lax.Precision.HIGHEST).astype(BF)
 
     low_mine = lax.dynamic_index_in_dim(total, me_e, 0, keepdims=False)[n_feat:]
-    low_all = lax.all_gather(low_mine, ("x", "y"), axis=0, tiled=False).reshape(RANK, slots)
+    low_all = lax.all_to_all(
+        jnp.broadcast_to(low_mine[None], (nxy,) + low_mine.shape),
+        ("x", "y"),
+        split_axis=0,
+        concat_axis=0,
+        tiled=True,
+    ).reshape(RANK, slots)
     tiled = jnp.tile(low_all, (TEN, 1))
     up_coef = (SCALE * flags * tiled.T).astype(BF)
     local = lax.dynamic_index_in_dim(

time: 213 us -> 154 us (0.72)
  the two profiles are of different devices: /device:TPU:32 before, /device:TPU:2 now
where the time goes in v2:
time: 154 us; the launch traced here: 153 us
  blocking collectives  68.6 us (45%)
  waiting for transfers between devices  34.5 us (22%)
  starting transfers between devices  31.2 us (20%)
  local copies, waits for them, and re-layouts  8.97 us (6%)
  matrix products  4.51 us (3%)
  other arithmetic  2.56 us (2%)
  Pallas kernels  2.19 us (1%)
    all_to_all x1, blocking collectives, on_device(): lax.all_to_all(jnp.broadcast_to(block[None], (nxy, quarter_rows, 2 * widt...  27.1 us
    all_to_all x1, blocking collectives, on_device(): lax.all_to_all(send.reshape(ne, part, -1), 'e', split_axis=0, concat_axis...  23.9 us
    all_to_all x1, waiting for transfers between devices, on_device(): lax.all_to_all(outgoing, ('zh', 'e'), split_axis=0, concat_axis=0, tiled=...  23.6 us
    all_to_all x1, starting transfers between devices, on_device(): lax.all_to_all(outgoing, ('zh', 'e'), split_axis=0, concat_axis=0, tiled=...  21.2 us
    all_to_all x1, blocking collectives, on_device(): lax.all_to_all(pair, ('x', 'y'), split_axis=0, concat_axis=0, tiled=True)  17.5 us
    all_to_all x1, starting transfers between devices, on_device(): lax.all_to_all(jnp.broadcast_to(low_mine[None], (nxy,) + low_mine.shape),...  6.03 us
    all_to_all x1, waiting for transfers between devices, on_device(): lax.all_to_all(jnp.broadcast_to(low_mine[None], (nxy,) + low_mine.shape),...  5.14 us
    unnamed x12, local copies, waits for them, and re-layouts  4.64 us
  transfers between devices with their start and end apart: 4, of which 4 were waited for; matrix products, arithmetic and copies ran while one was open for 1% of the time, Pallas kernels for 0%

profile of v2, /device:TPU:2, one launch (start us, length us, event | category | flops | bytes accessed | tf_op | source)
XLA Modules:
  0.0 153.3 jit_solution(13377735425459470431)
XLA Ops:
  0.6 0.8 slice_bitcast_fusion.4
  1.4 0.1 select_reduce_fusion
  1.5 0.8 fusion.51
  2.3 0.7 slice_bitcast_fusion.1
  3.1 0.7 multiply_add_fusion
  3.7 0.3 fusion.23
  4.0 0.3 fusion.1
  4.3 0.1 copy.31
  4.4 1.2 convolution_convert_fusion
  5.6 23.9 %all_to_all.25 = bf16[8,8,896]{2,1,0:T(8,128)(2,1)S(1)} all-to-all(bf16[8,8,896]{2,1,0:T(8,128)(2,1)S(1)} %fusion.9), channel_id=1, replica_groups=mesh['zh'=4,'x'=4,'e'=8,'y'=4,'c'=2] {'e'}, dimensions={0} | all-to-all | bytes 229376 | tf_op jit(solution)/shard_map/all_to_all | solution.py:151
  29.5 0.1 broadcast_in_dim.36
  29.7 0.0 copy-start.4
  29.7 27.1 %all_to_all.26.own = bf16[16,64,768]{2,1,0:T(8,128)(2,1)S(1)} all-to-all(bf16[16,64,768]{2,1,0:T(8,128)(2,1)S(1)} %broadcast_in_dim.36), channel_id=1, replica_groups=mesh['zh'=4,'x'=4,'e'=8,'y'=4,'c'=2] {'y','x'}, dimensions={0} | all-to-all | bytes 3145728 | tf_op jit(solution)/shard_map/all_to_all | solution.py:157
  56.9 1.9 %collective-permute-start = (bf16[16,64,768]{2,1,0:T(8,128)(2,1)S(1)}, bf16[16,64,768]{2,1,0:T(8,128)(2,1)S(1)}, u32[]{:S(2)}, u32[]{:S(2)}) collective-permute-start(bf16[16,64,768]{2,1,0:T(8,128)(2,1)S(1)} %all_to_all.26.own), channel_id=1, source_target_pairs={{0,1},{1,0},{2,3},{3,2},{4,5},{5,4},{6,7},{7,6},{8,9},{9,8},{10,11... | collective-permute-start | bytes 4718600 | tf_op jit(solution)/shard_map/ppermute | solution.py:164
  58.8 3.4 %collective-permute-done.other = bf16[16,64,768]{2,1,0:T(8,128)(2,1)S(1)} collective-permute-done((bf16[16,64,768]{2,1,0:T(8,128)(2,1)S(1)}, bf16[16,64,768]{2,1,0:T(8,128)(2,1)S(1)}, u32[]{:S(2)}, u32[]{:S(2)}) %collective-permute-start) | collective-permute-done | bytes 1572896 | tf_op jit(solution)/shard_map/ppermute | solution.py:164
  62.1 0.0 copy-done.4
  62.1 0.0 copy-start
  62.2 1.1 copy-done
  63.3 0.0 copy-start.1
  63.3 1.1 copy-done.1
  64.4 0.0 copy-start.2
  64.4 1.1 copy-done.2
  65.6 0.0 copy-start.3
  65.6 1.1 copy-done.3
  66.7 2.2 %shard_map.121 = (f32[16,112,256]{2,1,0:T(8,128)S(1)}, bf16[16,112,256]{2,1,0:T(8,128)(2,1)S(1)}, bf16[256,128]{1,0:T(8,128)(2,1)S(1)}, bf16[256,128]{1,0:T(8,128)(2,1)S(1)}, f32[256,128]{1,0:T(8,128)S(1)}) custom-call(s32[1]{0:T(128)} %bitcast.6.core, bf16[16,64,768]{2,1,0:T(8,128)(2,1)S(1)} %all_to_all.26.own, ...), custom_call_target="tpu_custom_call" | custom-call | flops 1006632960 | bytes 9437184 | tf_op jit(solution)/shard_map/pallas_call | solution.py:168
  68.9 2.0 %collective-permute-start.1 = (bf16[16,112,256]{2,1,0:T(8,128)(2,1)S(1)}, bf16[16,112,256]{2,1,0:T(8,128)(2,1)S(1)}, u32[]{:S(2)}, u32[]{:S(2)}) collective-permute-start(bf16[16,112,256]{2,1,0:T(8,128)(2,1)S(1)} %get-tuple-element.9), channel_id=1, source_target_pairs={{0,1},{1,0},{2,3},{3,2},{4,5},{5,4},{6,7},{7,6},{8,9},{9,8},{10,11... | collective-permute-start | bytes 2752520 | tf_op jit(solution)/shard_map/ppermute | solution.py:196
  70.9 2.3 %collective-permute-done.1 = bf16[16,112,256]{2,1,0:T(8,128)(2,1)S(1)} collective-permute-done((bf16[16,112,256]{2,1,0:T(8,128)(2,1)S(1)}, bf16[16,112,256]{2,1,0:T(8,128)(2,1)S(1)}, u32[]{:S(2)}, u32[]{:S(2)}) %collective-permute-start.1) | collective-permute-done | bytes 917536 | tf_op jit(solution)/shard_map/ppermute | solution.py:196
  73.2 0.3 fusion
  73.5 17.5 %all_to_all.27 = bf16[16,104,256]{2,1,0:T(8,128)(2,1)S(1)} all-to-all(bf16[16,104,256]{2,1,0:T(8,128)(2,1)S(1)} %fusion), channel_id=1, replica_groups=mesh['zh'=4,'x'=4,'e'=8,'y'=4,'c'=2] {'x','y'}, dimensions={0} | all-to-all | bytes 1703936 | tf_op jit(solution)/shard_map/all_to_all | solution.py:198
  91.1 0.1 reduce_sum.41
  91.2 0.1 copy.27
  91.3 0.2 reshape.228
  91.5 0.6 copy.28
  92.1 0.8 reshape.229
  93.0 0.7 pad_maximum_fusion
  93.6 21.2 %all-to-all-start.3 = ((bf16[32,8,128]{2,1,0:T(8,128)(2,1)}), bf16[32,8,128]{2,1,0:T(8,128)(2,1)S(1)}, u32[]{:S(2)}, u32[]{:S(2)}) async-start(bf16[32,8,128]{2,1,0:T(8,128)(2,1)} %pad_maximum_fusion), calls=%async_computation.3 | async-start | bytes 131072 | tf_op jit(solution)/shard_map/all_to_all | solution.py:208
  114.9 0.8 convolution_bitcast_fusion.1
  115.7 23.6 %all-to-all-done.3 = bf16[32,8,128]{2,1,0:T(8,128)(2,1)S(1)} async-done(((bf16[32,8,128]{2,1,0:T(8,128)(2,1)}), bf16[32,8,128]{2,1,0:T(8,128)(2,1)S(1)}, u32[]{:S(2)}, u32[]{:S(2)}) %all-to-all-start.3) | async-done | bytes 65568 | tf_op jit(solution)/shard_map/all_to_all | solution.py:208
  139.4 0.6 broadcast_in_dim.41
  140.0 6.0 %all-to-all-start.4 = ((f32[16,2,128]{2,1,0:T(2,128)}), f32[16,2,128]{2,1,0:T(2,128)S(1)}, u32[]{:S(2)}, u32[]{:S(2)}) async-start(f32[16,2,128]{2,1,0:T(2,128)} %broadcast_in_dim.41), calls=%async_computation.4 | async-start | bytes 32768 | tf_op jit(solution)/shard_map/all_to_all | solution.py:216
  146.1 0.1 reshape.230
  146.2 0.1 reshape.231
  146.3 0.9 convolution_convert_fusion.1
  147.1 5.1 %all-to-all-done.4 = f32[16,2,128]{2,1,0:T(2,128)S(1)} async-done(((f32[16,2,128]{2,1,0:T(2,128)}), f32[16,2,128]{2,1,0:T(2,128)S(1)}, u32[]{:S(2)}, u32[]{:S(2)}) %all-to-all-start.4) | async-done | bytes 16416 | tf_op jit(solution)/shard_map/all_to_all | solution.py:216
  152.3 0.1 copy.30
  152.4 0.9 convolution_bitcast_fusion
  (14 shorter events, 0.2 us)
Async XLA Ops:
  29.7 32.5 %copy-start.4 = (bf16[1,128,128]{2,1,0:T(8,128)(2,1)S(1)}, bf16[1,128,128]{2,1,0:T(8,128)(2,1)}, u32[]{:S(2)}) copy-start(bf16[1,128,128]{2,1,0:T(8,128)(2,1)} %param.18) | copy-start | bytes 98308
  56.9 5.3 %collective-permute-start = (bf16[16,64,768]{2,1,0:T(8,128)(2,1)S(1)}, bf16[16,64,768]{2,1,0:T(8,128)(2,1)S(1)}, u32[]{:S(2)}, u32[]{:S(2)}) collective-permute-start(bf16[16,64,768]{2,1,0:T(8,128)(2,1)S(1)} %all_to_all.26.own), channel_id=1, source_target_pairs={{0,1},{1,0},{2,3},{3,2},{4,5},{5,4},{6,7},{7,6},{8,9},{9,8},{10,11... | collective-permute-start | bytes 4718600 | tf_op jit(solution)/shard_map/ppermute | solution.py:164
  62.1 1.1 copy-start
  63.3 1.1 copy-start.1
  64.4 1.1 copy-start.2
  65.6 1.1 copy-start.3
  68.9 4.4 %collective-permute-start.1 = (bf16[16,112,256]{2,1,0:T(8,128)(2,1)S(1)}, bf16[16,112,256]{2,1,0:T(8,128)(2,1)S(1)}, u32[]{:S(2)}, u32[]{:S(2)}) collective-permute-start(bf16[16,112,256]{2,1,0:T(8,128)(2,1)S(1)} %get-tuple-element.9), channel_id=1, source_target_pairs={{0,1},{1,0},{2,3},{3,2},{4,5},{5,4},{6,7},{7,6},{8,9},{9,8},{10,11... | collective-permute-start | bytes 2752520 | tf_op jit(solution)/shard_map/ppermute | solution.py:196
  93.6 45.8 %all-to-all-start.3 = ((bf16[32,8,128]{2,1,0:T(8,128)(2,1)}), bf16[32,8,128]{2,1,0:T(8,128)(2,1)S(1)}, u32[]{:S(2)}, u32[]{:S(2)}) async-start(bf16[32,8,128]{2,1,0:T(8,128)(2,1)} %pad_maximum_fusion), calls=%async_computation.3 | async-start | bytes 131072 | tf_op jit(solution)/shard_map/all_to_all | solution.py:208
  140.0 12.2 %all-to-all-start.4 = ((f32[16,2,128]{2,1,0:T(2,128)}), f32[16,2,128]{2,1,0:T(2,128)S(1)}, u32[]{:S(2)}, u32[]{:S(2)}) async-start(f32[16,2,128]{2,1,0:T(2,128)} %broadcast_in_dim.41), calls=%async_computation.4 | async-start | bytes 32768 | tf_op jit(solution)/shard_map/all_to_all | solution.py:216

commit v3 on v2

--- a/solution.py
+++ b/solution.py
@@ -21,15 +21,41 @@
     )
 
 
-def hot(index, size):
-    return lax.broadcasted_iota(jnp.int32, (index.shape[0], size), 1) == index
+def dispatch_kernel(nx, ne, where, ids, probs, tenants, tokens, cotangent, send, combine):
+    group, width = tokens.shape
+    part = CAP // nx
+    shift = part.bit_length() - 1
+    rank_in = functools.partial(lax.broadcasted_iota, jnp.int32)
+    named = [rank_in((ne, group), 0) == ids[j : j + 1, :] for j in range(2)]
+    either = (named[0] | named[1]).astype(F32).astype(BF)
+    before = (rank_in((group, group), 0) < rank_in((group, group), 1)).astype(F32).astype(BF)
+    earlier = dot(either, before, 1, 0)
+    pick, marks, back = None, None, None
+    for j in range(2):
+        expert = ids[j : j + 1, :]
+        slot = jnp.sum(jnp.where(named[j], earlier, 0.0), axis=0, keepdims=True).astype(jnp.int32)
+        quarter, rest = slot >> shift, slot & (part - 1)
+        here = rank_in((ne * part, group), 0) == expert * part + rest
+        mine = jnp.where(here & (quarter == where[0]), 1.0, 0.0)
+        weighted = jnp.where(here, probs[j : j + 1, :].astype(F32), 0.0).astype(BF)
+        column = rank_in((128, group), 0) == quarter * TEN + tenants[...]
+        mark = dot(weighted, jnp.where(column, 1.0, 0.0).astype(BF), 1, 1)
+        home = jnp.where(rank_in((ne * CAP, group), 0) == expert * CAP + slot, 1.0, 0.0)
+        pick = mine if pick is None else pick + mine
+        marks = mark if marks is None else marks + mark
+        back = home if back is None else back + home
+    pick = pick.astype(BF)
+    rows = [dot(pick, tokens[...], 1, 0), dot(pick, cotangent[...], 1, 0), marks]
+    rows = jnp.concatenate(rows, 1).reshape(ne, part, 2 * width + 128)
+    send[...] = rows.astype(BF)
+    combine[...] = back
 
 
 def expert_kernel(
     sizes, core, own, other, held_marks, gate_mat, up_mat, down_mat, first, second,
     keep, give, hidden_out, down_out, flags_out, terms,
 ):
-    nz, nx, ny, nc = sizes
+    nz, nx, ny, nc, ne = sizes
     nxy = nx * ny
     mine = core[0]
     quarter_rows, width = own.shape[1], own.shape[2] // 2
@@ -70,13 +96,16 @@
     down_coef = (SCALE * flags * low_back).astype(BF)
     hidden_grad = weight * back_acc + dot(down_coef, first[...], 1, 1)
     slope = sig * (1.0 + gate_acc * (1.0 - sig))
-    gate_grad = (hidden_grad * up_acc * slope).astype(BF)
-    up_grad = (hidden_grad * silu).astype(BF)
+    gate_grad = hidden_grad * up_acc * slope
+    up_grad = hidden_grad * silu
     hidden_out[...] = hidden
     down_out[...] = down_coef
     flags_out[...] = flags
 
     grads = jnp.concatenate([gate_grad, up_grad], 1)
+    size = quarter_rows // ne
+    starts = [x * quarter_rows + e * size for e in range(ne) for x in range(nx)]
+    grads = jnp.concatenate([grads[at : at + size] for at in starts], 0).astype(BF)
     for z in range(nz):
         at = slice(z * part, (z + 1) * part)
         mats = jnp.concatenate([gate_mat[at, :], up_mat[at, :]], 1)
@@ -86,14 +115,13 @@
     fold = (rank_of == lax.broadcasted_iota(jnp.int32, (RANK, low_width), 0)).astype(BF)
     kept = jnp.where(flags != 0.0, low_part, 0.0).astype(BF)
     low_rows = dot(fold, kept, 1, 1)
-    under = lax.broadcasted_iota(jnp.int32, (16, slots), 0) == 0
     for p in range(nxy):
         for out, at_core in ((keep, mine), (give, 1 - mine)):
             chunks = [
                 terms[pl.ds(pl.multiple_of(z * part + (p * nc + at_core) * piece, 8), piece), :]
                 for z in range(nz)
             ]
-            chunks.append(jnp.where(under, low_rows[p : p + 1, :], 0.0))
+            chunks.append(low_rows)
             out[p] = jnp.concatenate(chunks, 0).astype(out.dtype)
 
 
@@ -114,43 +142,33 @@
     group, width = tokens.shape
     slots = ne * CAP
     part = CAP // nx
-    me_x, me_e, me_y, me_c = (lax.axis_index(a) for a in ("x", "e", "y", "c"))
+    me_x, me_y, me_c = (lax.axis_index(a) for a in ("x", "y", "c"))
     swap = [(0, 1), (1, 0)]
     gate_mat, up_mat, down_mat = w_gate[0], w_up[0], w_down[0]
     first, second = adapter_in[0], adapter_out[0]
     features = gate_mat.shape[0]
     piece = features // (nz * nxy * nc)
 
-    named = [hot(expert_ids[:, j : j + 1], ne) for j in range(2)]
-    either = (named[0] | named[1]).astype(BF)
-    before = (
-        lax.broadcasted_iota(jnp.int32, (group, group), 1)
-        < lax.broadcasted_iota(jnp.int32, (group, group), 0)
-    ).astype(BF)
-    earlier = dot(before, either, 1, 0)
-    slot = [
-        jnp.sum(jnp.where(n, earlier, 0.0), axis=1, keepdims=True).astype(jnp.int32) for n in named
-    ]
-    tenant = tenant_ids[:, None]
-
-    pick, marks, combine = None, None, None
-    for j in range(2):
-        expert = expert_ids[:, j : j + 1]
-        quarter, rest = slot[j] // part, slot[j] % part
-        here = hot(expert * part + rest, ne * part)
-        mine = (here & (quarter == me_x)).astype(BF)
-        weighted = here.astype(BF) * gate_probs[:, j : j + 1]
-        mark = dot(weighted, hot(quarter * TEN + tenant, nx * TEN).astype(BF), 0, 0)
-        back = hot(expert * CAP + slot[j], slots).astype(F32)
-        pick = mine if pick is None else pick + mine
-        marks = mark if marks is None else marks + mark
-        combine = back if combine is None else combine + back
-    rows = dot(pick, jnp.concatenate([tokens, cotangent], axis=1), 0, 0).astype(BF)
-    pad = -(nx * TEN) % 128
-    send = jnp.concatenate([rows, jnp.pad(marks.astype(BF), ((0, 0), (0, pad)))], axis=1)
-    held = lax.all_to_all(
-        send.reshape(ne, part, -1), "e", split_axis=0, concat_axis=0, tiled=True
-    ).reshape(ne * part, -1)
+    in_vmem = pl.BlockSpec(memory_space=pltpu.VMEM)
+    in_smem = pl.BlockSpec(memory_space=pltpu.SMEM)
+    send, combine = pl.pallas_call(
+        functools.partial(dispatch_kernel, nx, ne),
+        out_shape=(
+            jax.ShapeDtypeStruct((ne, part, 2 * width + 128), BF),
+            jax.ShapeDtypeStruct((slots, group), F32),
+        ),
+        in_specs=[in_smem] + [in_vmem] * 5,
+        out_specs=(in_vmem,) * 2,
+    )(
+        me_x.reshape(1).astype(jnp.int32),
+        expert_ids.T,
+        gate_probs.T,
+        tenant_ids[None],
+        tokens,
+        cotangent,
+    )
+    held = lax.all_to_all(send, "e", split_axis=0, concat_axis=0, tiled=True)
+    held = held.reshape(ne * part, -1)
 
     quarter_rows = ne * part
     block = held[:, : 2 * width]
@@ -163,10 +181,9 @@
     )
     other = lax.ppermute(own, "c", swap)
     units, low_width = gate_mat.shape[1], first.shape[1]
-    tall = nz * piece + 16
-    in_vmem = pl.BlockSpec(memory_space=pltpu.VMEM)
+    tall = nz * piece + RANK
     keep, give, hidden, down_coef, flags = pl.pallas_call(
-        functools.partial(expert_kernel, (nz, nx, ny, nc)),
+        functools.partial(expert_kernel, (nz, nx, ny, nc, ne)),
         out_shape=(
             jax.ShapeDtypeStruct((nxy, tall, slots), F32),
             jax.ShapeDtypeStruct((nxy, tall, slots), BF),
@@ -174,7 +191,7 @@
             jax.ShapeDtypeStruct((slots, low_width), BF),
             jax.ShapeDtypeStruct((slots, low_width), F32),
         ),
-        in_specs=[pl.BlockSpec(memory_space=pltpu.SMEM)] + [in_vmem] * 8,
+        in_specs=[in_smem] + [in_vmem] * 8,
         out_specs=(in_vmem,) * 5,
         scratch_shapes=[pltpu.VMEM((features, slots), F32)],
         compiler_params=pltpu.CompilerParams(vmem_limit_bytes=40 << 20),
@@ -193,33 +210,34 @@
         second,
     )
     grad_a = dot(hidden, down_coef, 0, 0)
-    pair = keep + lax.ppermute(give, "c", swap).astype(F32)
-    pair = pair[:, : nz * piece + 8].astype(BF)
+    pair = (keep + lax.ppermute(give, "c", swap).astype(F32)).astype(BF)
     plane = lax.all_to_all(pair, ("x", "y"), split_axis=0, concat_axis=0, tiled=True)
-    plane = jnp.sum(plane.astype(F32), axis=0).astype(BF)
-
-    feats = plane[: nz * piece].reshape(nz, piece, nx, ne, part).transpose(0, 3, 1, 2, 4)
+    plane = jnp.sum(plane.astype(F32), axis=0)
+
+    def share(z):
+        return jnp.concatenate(
+            [lax.dynamic_slice_in_dim(plane, z * piece, piece, 0), plane[nz * piece :]], axis=0
+        )
+
+    me_z = lax.axis_index("zh")
+    total = share(me_z)
+    for k in sorted(range(1, nz), key=lambda k: -min(k, nz - k)):
+        block = share((me_z + k) % nz).astype(BF)
+        total += lax.ppermute(block, "zh", [(i, (i + k) % nz) for i in range(nz)]).astype(F32)
+
     lanes = 128
-    feats = feats.reshape(nz * ne, piece * CAP // lanes, lanes)
-    low_line = plane[nz * piece].reshape(1, slots // lanes, lanes)
-    outgoing = jnp.concatenate(
-        [feats, jnp.broadcast_to(low_line, (nz * ne, slots // lanes, lanes))], axis=1
-    )
-    came = lax.all_to_all(outgoing, ("zh", "e"), split_axis=0, concat_axis=0, tiled=True)
-    came = came.reshape(nz, ne, -1, lanes)
-    n_feat = piece * CAP // lanes
-    total = jnp.sum(came.astype(F32), axis=0)
-    returned = total[:, :n_feat].reshape(ne, piece, CAP).transpose(1, 0, 2).reshape(piece, slots)
-    input_grad = dot(combine, returned, 1, 1, lax.Precision.HIGHEST).astype(BF)
-
-    low_mine = lax.dynamic_index_in_dim(total, me_e, 0, keepdims=False)[n_feat:]
-    low_all = lax.all_to_all(
-        jnp.broadcast_to(low_mine[None], (nxy,) + low_mine.shape),
-        ("x", "y"),
+    feats = total[:piece].reshape(piece, ne, CAP).transpose(1, 0, 2)
+    came = lax.all_to_all(
+        feats.reshape(ne, piece * CAP // lanes, lanes),
+        "e",
         split_axis=0,
         concat_axis=0,
         tiled=True,
-    ).reshape(RANK, slots)
+    )
+    returned = came.reshape(ne, piece, CAP).transpose(1, 0, 2).reshape(piece, slots)
+    input_grad = dot(combine, returned, 0, 1, lax.Precision.HIGHEST).astype(BF)
+
+    low_all = total[piece:]
     tiled = jnp.tile(low_all, (TEN, 1))
     up_coef = (SCALE * flags * tiled.T).astype(BF)
     local = lax.dynamic_index_in_dim(

time: 154 us -> 152 us (0.987)
  the two profiles are of different devices: /device:TPU:2 before, /device:TPU:8 now
where the time goes in v3:
time: 152 us
  starting transfers between devices  51.1 us (34%)
  blocking collectives  50.2 us (33%)
  waiting for transfers between devices  35.5 us (23%)
  local copies, waits for them, and re-layouts  5.86 us (4%)
  Pallas kernels  4.22 us (3%)
  matrix products  2.51 us (2%)
    ppermute x3, starting transfers between devices, on_device(): lax.ppermute(block, 'zh', [(i, (i + k) % nz) for i in range(nz)])  36 us
    all_to_all x1, blocking collectives, on_device(): lax.all_to_all(jnp.broadcast_to(block[None], (nxy, quarter_rows, 2 * widt...  26.1 us
    all_to_all x1, blocking collectives, on_device(): held = lax.all_to_all(send, 'e', split_axis=0, concat_axis=0, tiled=True)  24.1 us
    all_to_all x1, waiting for transfers between devices, on_device(): lax.all_to_all(pair, ('x', 'y'), split_axis=0, concat_axis=0, tiled=True)  15.5 us
    all_to_all x1, waiting for transfers between devices, on_device(): lax.all_to_all(feats.reshape(ne, piece * CAP // lanes, lanes), 'e', split...  8.8 us
    all_to_all x1, starting transfers between devices, on_device(): lax.all_to_all(pair, ('x', 'y'), split_axis=0, concat_axis=0, tiled=True)  5.8 us
    ppermute x3, waiting for transfers between devices, on_device(): lax.ppermute(block, 'zh', [(i, (i + k) % nz) for i in range(nz)])  5.56 us
    all_to_all x1, starting transfers between devices, on_device(): lax.all_to_all(feats.reshape(ne, piece * CAP // lanes, lanes), 'e', split...  5.28 us
  transfers between devices with their start and end apart: 7, of which 5 were waited for; matrix products, arithmetic and copies ran while one was open for 1% of the time, Pallas kernels for 0%

profile of v3, /device:TPU:8, one launch (start us, length us, event | category | flops | bytes accessed | tf_op | source)
XLA Modules:
  0.0 151.6 jit_solution(4815564262973802554)
XLA Ops:
  0.6 2.0 %shard_map.121 = (bf16[8,8,896]{2,1,0:T(8,128)(2,1)}, f32[256,96]{1,0:T(8,128)}) custom-call(s32[1]{0:T(128)} %bitcast.where, s32[2,96]{1,0:T(2,128)} %bitcast.41, bf16[2,96]{1,0:T(2,128)(2,1)} %bitcast.42, s32[1,96]{1,0:T(1,128)} %bitcast.43, bf16[96,384]{1,0:T(8,128)(2,1)} %tokens.1, bf16[96,384]{1,0:T(8,128)(2,1)} %cotangent.1), custom_call_target="tpu_custom_call" | custom-call | tf_op jit(solution)/shard_map/pallas_call | solution.py:154
  2.6 24.1 %all_to_all.20 = bf16[8,8,896]{2,1,0:T(8,128)(2,1)S(1)} all-to-all(bf16[8,8,896]{2,1,0:T(8,128)(2,1)} %get-tuple-element.11), channel_id=1, replica_groups=mesh['zh'=4,'x'=4,'e'=8,'y'=4,'c'=2] {'e'}, dimensions={0} | all-to-all | bytes 229376 | tf_op jit(solution)/shard_map/all_to_all | solution.py:170
  26.7 0.1 broadcast_in_dim.16
  26.9 0.0 copy-start.4
  26.9 26.1 %all_to_all.21.own = bf16[16,64,768]{2,1,0:T(8,128)(2,1)S(1)} all-to-all(bf16[16,64,768]{2,1,0:T(8,128)(2,1)S(1)} %broadcast_in_dim.16), channel_id=1, replica_groups=mesh['zh'=4,'x'=4,'e'=8,'y'=4,'c'=2] {'y','x'}, dimensions={0} | all-to-all | bytes 3145728 | tf_op jit(solution)/shard_map/all_to_all | solution.py:175
  53.0 1.9 %collective-permute-start = (bf16[16,64,768]{2,1,0:T(8,128)(2,1)S(1)}, bf16[16,64,768]{2,1,0:T(8,128)(2,1)S(1)}, u32[]{:S(2)}, u32[]{:S(2)}) collective-permute-start(bf16[16,64,768]{2,1,0:T(8,128)(2,1)S(1)} %all_to_all.21.own), channel_id=1, source_target_pairs={{0,1},{1,0},{2,3},{3,2},{4,5},{5,4},{6,7},{7,6},{8,9},{9,8},{10,11... | collective-permute-start | bytes 4718600 | tf_op jit(solution)/shard_map/ppermute | solution.py:182
  54.9 3.4 %collective-permute-done.other = bf16[16,64,768]{2,1,0:T(8,128)(2,1)S(1)} collective-permute-done((bf16[16,64,768]{2,1,0:T(8,128)(2,1)S(1)}, bf16[16,64,768]{2,1,0:T(8,128)(2,1)S(1)}, u32[]{:S(2)}, u32[]{:S(2)}) %collective-permute-start) | collective-permute-done | bytes 1572896 | tf_op jit(solution)/shard_map/ppermute | solution.py:182
  58.3 0.0 copy-done.4
  58.3 0.0 copy-start
  58.3 1.1 copy-done
  59.4 0.0 copy-start.1
  59.4 1.1 copy-done.1
  60.6 0.0 copy-start.2
  60.6 1.1 copy-done.2
  61.7 0.0 copy-start.3
  61.7 1.1 copy-done.3
  62.8 2.2 %shard_map.122 = (f32[16,112,256]{2,1,0:T(8,128)S(1)}, bf16[16,112,256]{2,1,0:T(8,128)(2,1)S(1)}, bf16[256,128]{1,0:T(8,128)(2,1)S(1)}, bf16[256,128]{1,0:T(8,128)(2,1)S(1)}, f32[256,128]{1,0:T(8,128)S(1)}) custom-call(s32[1]{0:T(128)} %bitcast.4.core, bf16[16,64,768]{2,1,0:T(8,128)(2,1)S(1)} %all_to_all.21.own, ...), custom_call_target="tpu_custom_call" | custom-call | flops 1006632960 | bytes 9437184 | tf_op jit(solution)/shard_map/pallas_call | solution.py:185
  65.1 2.0 %collective-permute-start.1 = (bf16[16,112,256]{2,1,0:T(8,128)(2,1)S(1)}, bf16[16,112,256]{2,1,0:T(8,128)(2,1)S(1)}, u32[]{:S(2)}, u32[]{:S(2)}) collective-permute-start(bf16[16,112,256]{2,1,0:T(8,128)(2,1)S(1)} %get-tuple-element.13), channel_id=1, source_target_pairs={{0,1},{1,0},{2,3},{3,2},{4,5},{5,4},{6,7},{7,6},{8,9},{9,8},{10,11... | collective-permute-start | bytes 2752520 | tf_op jit(solution)/shard_map/ppermute | solution.py:213
  67.2 2.3 %collective-permute-done.1 = bf16[16,112,256]{2,1,0:T(8,128)(2,1)S(1)} collective-permute-done((bf16[16,112,256]{2,1,0:T(8,128)(2,1)S(1)}, bf16[16,112,256]{2,1,0:T(8,128)(2,1)S(1)}, u32[]{:S(2)}, u32[]{:S(2)}) %collective-permute-start.1) | collective-permute-done | bytes 917536 | tf_op jit(solution)/shard_map/ppermute | solution.py:213
  69.5 1.2 add_convert_fusion
  70.7 5.8 %all-to-all-start.2 = ((bf16[16,112,256]{2,1,0:T(8,128)(2,1)}), bf16[16,112,256]{2,1,0:T(8,128)(2,1)S(1)}, u32[]{:S(2)}, u32[]{:S(2)}) async-start(bf16[16,112,256]{2,1,0:T(8,128)(2,1)} %add_convert_fusion), calls=%async_computation.2 | async-start | bytes 1835008 | tf_op jit(solution)/shard_map/all_to_all | solution.py:214
  76.5 0.0 copy-start.5
  76.5 15.5 %all-to-all-done.2 = bf16[16,112,256]{2,1,0:T(8,128)(2,1)S(1)} async-done(((bf16[16,112,256]{2,1,0:T(8,128)(2,1)}), bf16[16,112,256]{2,1,0:T(8,128)(2,1)S(1)}, u32[]{:S(2)}, u32[]{:S(2)}) %all-to-all-start.2) | async-done | bytes 917536 | tf_op jit(solution)/shard_map/all_to_all | solution.py:214
  92.0 0.1 convert_reduce_fusion
  92.2 15.5 %collective-permute-start.4 = (bf16[40,256]{1,0:T(8,128)(2,1)S(1)}, bf16[40,256]{1,0:T(8,128)(2,1)S(1)}, u32[]{:S(2)}, u32[]{:S(2)}) collective-permute-start(bf16[40,256]{1,0:T(8,128)(2,1)S(1)} %get-tuple-element.22), channel_id=1, source_target_pairs={{0,768},{256,0},{512,256},{768,512},{1,769},{257,1},{513,257},{769... | collective-permute-start | bytes 61448 | tf_op jit(solution)/shard_map/ppermute | solution.py:226
  107.7 2.1 %collective-permute-start.3 = (bf16[40,256]{1,0:T(8,128)(2,1)S(1)}, bf16[40,256]{1,0:T(8,128)(2,1)S(1)}, u32[]{:S(2)}, u32[]{:S(2)}) collective-permute-start(bf16[40,256]{1,0:T(8,128)(2,1)S(1)} %get-tuple-element.21), channel_id=1, source_target_pairs={{0,256},{256,512},{512,768},{768,0},{1,257},{257,513},{513,769},{7... | collective-permute-start | bytes 61448 | tf_op jit(solution)/shard_map/ppermute | solution.py:226
  109.8 18.4 %collective-permute-start.2 = (bf16[40,256]{1,0:T(8,128)(2,1)S(1)}, bf16[40,256]{1,0:T(8,128)(2,1)S(1)}, u32[]{:S(2)}, u32[]{:S(2)}) collective-permute-start(bf16[40,256]{1,0:T(8,128)(2,1)S(1)} %get-tuple-element.20), channel_id=1, source_target_pairs={{0,512},{256,768},{512,0},{768,256},{1,513},{257,769},{513,1},{769... | collective-permute-start | bytes 61448 | tf_op jit(solution)/shard_map/ppermute | solution.py:226
  128.3 0.0 collective-permute-done.4
  128.3 0.0 collective-permute-done.3
  128.3 5.6 %collective-permute-done.2 = bf16[40,256]{1,0:T(8,128)(2,1)S(1)} collective-permute-done((bf16[40,256]{1,0:T(8,128)(2,1)S(1)}, bf16[40,256]{1,0:T(8,128)(2,1)S(1)}, u32[]{:S(2)}, u32[]{:S(2)}) %collective-permute-start.2) | collective-permute-done | bytes 20512 | tf_op jit(solution)/shard_map/ppermute | solution.py:226
  133.9 0.1 reshape.38
  134.0 0.7 reshape.39
  134.7 5.3 %all-to-all-start.3 = ((f32[8,6,128]{2,1,0:T(8,128)}), f32[8,6,128]{2,1,0:T(8,128)S(1)}, u32[]{:S(2)}, u32[]{:S(2)}) async-start(f32[8,6,128]{2,1,0:T(8,128)} %reshape.39), calls=%async_computation.3 | async-start | bytes 65536 | tf_op jit(solution)/shard_map/all_to_all | solution.py:230
  140.0 0.8 convolution_bitcast_fusion.1
  140.8 0.1 copy.17
  140.9 0.9 convolution_bitcast_fusion
  141.8 8.8 %all-to-all-done.3 = f32[8,6,128]{2,1,0:T(8,128)S(1)} async-done(((f32[8,6,128]{2,1,0:T(8,128)}), f32[8,6,128]{2,1,0:T(8,128)S(1)}, u32[]{:S(2)}, u32[]{:S(2)}) %all-to-all-start.3) | async-done | bytes 24608 | tf_op jit(solution)/shard_map/all_to_all | solution.py:230
  150.6 0.1 reshape.40
  150.7 0.1 reshape.41
  150.8 0.0 copy-done.5
  150.8 0.8 convolution_convert_fusion
  (14 shorter events, 0.2 us)
Async XLA Ops:
  26.9 31.4 %copy-start.4 = (bf16[1,128,128]{2,1,0:T(8,128)(2,1)S(1)}, bf16[1,128,128]{2,1,0:T(8,128)(2,1)}, u32[]{:S(2)}) copy-start(bf16[1,128,128]{2,1,0:T(8,128)(2,1)} %param.18) | copy-start | bytes 98308
  53.0 5.3 %collective-permute-start = (bf16[16,64,768]{2,1,0:T(8,128)(2,1)S(1)}, bf16[16,64,768]{2,1,0:T(8,128)(2,1)S(1)}, u32[]{:S(2)}, u32[]{:S(2)}) collective-permute-start(bf16[16,64,768]{2,1,0:T(8,128)(2,1)S(1)} %all_to_all.21.own), channel_id=1, source_target_pairs={{0,1},{1,0},{2,3},{3,2},{4,5},{5,4},{6,7},{7,6},{8,9},{9,8},{10,11... | collective-permute-start | bytes 4718600 | tf_op jit(solution)/shard_map/ppermute | solution.py:182
  58.3 1.1 copy-start
  59.4 1.1 copy-start.1
  60.6 1.1 copy-start.2
  61.7 1.1 copy-start.3
  65.1 4.4 %collective-permute-start.1 = (bf16[16,112,256]{2,1,0:T(8,128)(2,1)S(1)}, bf16[16,112,256]{2,1,0:T(8,128)(2,1)S(1)}, u32[]{:S(2)}, u32[]{:S(2)}) collective-permute-start(bf16[16,112,256]{2,1,0:T(8,128)(2,1)S(1)} %get-tuple-element.13), channel_id=1, source_target_pairs={{0,1},{1,0},{2,3},{3,2},{4,5},{5,4},{6,7},{7,6},{8,9},{9,8},{10,11... | collective-permute-start | bytes 2752520 | tf_op jit(solution)/shard_map/ppermute | solution.py:213
  70.7 21.3 %all-to-all-start.2 = ((bf16[16,112,256]{2,1,0:T(8,128)(2,1)}), bf16[16,112,256]{2,1,0:T(8,128)(2,1)S(1)}, u32[]{:S(2)}, u32[]{:S(2)}) async-start(bf16[16,112,256]{2,1,0:T(8,128)(2,1)} %add_convert_fusion), calls=%async_computation.2 | async-start | bytes 1835008 | tf_op jit(solution)/shard_map/all_to_all | solution.py:214
  76.5 74.3 %copy-start.5 = (f32[256,96]{1,0:T(8,128)S(1)}, f32[256,96]{1,0:T(8,128)}, u32[]{:S(2)}) copy-start(f32[256,96]{1,0:T(8,128)} %get-tuple-element.10) | copy-start | bytes 294916
  92.2 36.1 %collective-permute-start.4 = (bf16[40,256]{1,0:T(8,128)(2,1)S(1)}, bf16[40,256]{1,0:T(8,128)(2,1)S(1)}, u32[]{:S(2)}, u32[]{:S(2)}) collective-permute-start(bf16[40,256]{1,0:T(8,128)(2,1)S(1)} %get-tuple-element.22), channel_id=1, source_target_pairs={{0,768},{256,0},{512,256},{768,512},{1,769},{257,1},{513,257},{769... | collective-permute-start | bytes 61448 | tf_op jit(solution)/shard_map/ppermute | solution.py:226
  107.7 20.6 %collective-permute-start.3 = (bf16[40,256]{1,0:T(8,128)(2,1)S(1)}, bf16[40,256]{1,0:T(8,128)(2,1)S(1)}, u32[]{:S(2)}, u32[]{:S(2)}) collective-permute-start(bf16[40,256]{1,0:T(8,128)(2,1)S(1)} %get-tuple-element.21), channel_id=1, source_target_pairs={{0,256},{256,512},{512,768},{768,0},{1,257},{257,513},{513,769},{7... | collective-permute-start | bytes 61448 | tf_op jit(solution)/shard_map/ppermute | solution.py:226
  109.8 24.0 %collective-permute-start.2 = (bf16[40,256]{1,0:T(8,128)(2,1)S(1)}, bf16[40,256]{1,0:T(8,128)(2,1)S(1)}, u32[]{:S(2)}, u32[]{:S(2)}) collective-permute-start(bf16[40,256]{1,0:T(8,128)(2,1)S(1)} %get-tuple-element.20), channel_id=1, source_target_pairs={{0,512},{256,768},{512,0},{768,256},{1,513},{257,769},{513,1},{769... | collective-permute-start | bytes 61448 | tf_op jit(solution)/shard_map/ppermute | solution.py:226
  134.7 15.9 %all-to-all-start.3 = ((f32[8,6,128]{2,1,0:T(8,128)}), f32[8,6,128]{2,1,0:T(8,128)S(1)}, u32[]{:S(2)}, u32[]{:S(2)}) async-start(f32[8,6,128]{2,1,0:T(8,128)} %reshape.39), calls=%async_computation.3 | async-start | bytes 65536 | tf_op jit(solution)/shard_map/all_to_all | solution.py:230

commit v4 on v3

--- a/solution.py
+++ b/solution.py
@@ -214,19 +214,25 @@
     plane = lax.all_to_all(pair, ("x", "y"), split_axis=0, concat_axis=0, tiled=True)
     plane = jnp.sum(plane.astype(F32), axis=0)
 
-    def share(z):
-        return jnp.concatenate(
-            [lax.dynamic_slice_in_dim(plane, z * piece, piece, 0), plane[nz * piece :]], axis=0
-        )
-
+    feats, low_own = plane[: nz * piece].reshape(nz, piece, slots), plane[nz * piece :]
     me_z = lax.axis_index("zh")
-    total = share(me_z)
-    for k in sorted(range(1, nz), key=lambda k: -min(k, nz - k)):
-        block = share((me_z + k) % nz).astype(BF)
-        total += lax.ppermute(block, "zh", [(i, (i + k) % nz) for i in range(nz)]).astype(F32)
+
+    def block(step):
+        return lax.dynamic_index_in_dim(feats, (me_z + step) % nz, 0, keepdims=False)
+
+    def pass_on(rows, low, step):
+        sent = jnp.concatenate([rows, low], axis=0).astype(BF)
+        got = lax.ppermute(sent, "zh", [(i, (i + step) % nz) for i in range(nz)]).astype(F32)
+        return got[:piece], got[piece:]
+
+    far_rows, low_below = pass_on(block(2), low_own, 1)
+    rows_above, low_above = pass_on(block(nz - 1), low_own, nz - 1)
+    rows_below, low_far = pass_on(block(1) + far_rows, low_below, 1)
+    total = block(0) + rows_above + rows_below
+    low_all = low_own + low_above + low_below + low_far
 
     lanes = 128
-    feats = total[:piece].reshape(piece, ne, CAP).transpose(1, 0, 2)
+    feats = total.reshape(piece, ne, CAP).transpose(1, 0, 2)
     came = lax.all_to_all(
         feats.reshape(ne, piece * CAP // lanes, lanes),
         "e",
@@ -237,7 +243,6 @@
     returned = came.reshape(ne, piece, CAP).transpose(1, 0, 2).reshape(piece, slots)
     input_grad = dot(combine, returned, 0, 1, lax.Precision.HIGHEST).astype(BF)
 
-    low_all = total[piece:]
     tiled = jnp.tile(low_all, (TEN, 1))
     up_coef = (SCALE * flags * tiled.T).astype(BF)
     local = lax.dynamic_index_in_dim(

time: 152 us -> 143 us (0.941)
  starting transfers between devices: 51.1 us -> 45.8 us
  waiting for transfers between devices: 35.5 us -> 31.7 us
    ppermute x3, starting transfers between devices: 36 us -> 30.4 us  [pass_on(): lax.ppermute(sent, 'zh', [(i, (i + step) % nz) for i in range(nz)])]
    ppermute x3, waiting for transfers between devices: 5.56 us -> 0.91 us  [pass_on(): lax.ppermute(sent, 'zh', [(i, (i + step) % nz) for i in range(nz)])]
where the time goes in v4:
time: 143 us
  blocking collectives  50.2 us (35%)
  starting transfers between devices  45.8 us (32%)
  waiting for transfers between devices  31.7 us (22%)
  local copies, waits for them, and re-layouts  5.86 us (4%)
  Pallas kernels  4.22 us (3%)
  matrix products  2.51 us (2%)
    ppermute x3, starting transfers between devices, pass_on(): lax.ppermute(sent, 'zh', [(i, (i + step) % nz) for i in range(nz)])  30.4 us
    all_to_all x1, blocking collectives, on_device(): lax.all_to_all(jnp.broadcast_to(block[None], (nxy, quarter_rows, 2 * widt...  26.1 us
    all_to_all x1, blocking collectives, on_device(): held = lax.all_to_all(send, 'e', split_axis=0, concat_axis=0, tiled=True)  24.1 us
    all_to_all x1, waiting for transfers between devices, on_device(): lax.all_to_all(pair, ('x', 'y'), split_axis=0, concat_axis=0, tiled=True)  15.5 us
    all_to_all x1, waiting for transfers between devices, on_device(): lax.all_to_all(feats.reshape(ne, piece * CAP // lanes, lanes), 'e', split...  9.61 us
    all_to_all x1, starting transfers between devices, on_device(): lax.all_to_all(pair, ('x', 'y'), split_axis=0, concat_axis=0, tiled=True)  5.8 us
    all_to_all x1, starting transfers between devices, on_device(): lax.all_to_all(feats.reshape(ne, piece * CAP // lanes, lanes), 'e', split...  5.64 us
    unnamed x12, local copies, waits for them, and re-layouts  4.54 us
  transfers between devices with their start and end apart: 7, of which 5 were waited for; matrix products, arithmetic and copies ran while one was open for 1% of the time, Pallas kernels for 0%

profile of v4, /device:TPU:8, one launch (start us, length us, event | category | flops | bytes accessed | tf_op | source)
XLA Modules:
  0.0 142.6 jit_solution(4703320433351633059)
XLA Ops:
  0.6 2.0 %shard_map.121 = (bf16[8,8,896]{2,1,0:T(8,128)(2,1)}, f32[256,96]{1,0:T(8,128)}) custom-call(s32[1]{0:T(128)} %bitcast.where, s32[2,96]{1,0:T(2,128)} %bitcast.55, bf16[2,96]{1,0:T(2,128)(2,1)} %bitcast.56, s32[1,96]{1,0:T(1,128)} %bitcast.57, bf16[96,384]{1,0:T(8,128)(2,1)} %tokens.1, bf16[96,384]{1,0:T(8,128)(2,1)} %cotangent.1), custom_call_target="tpu_custom_call" | custom-call | tf_op jit(solution)/shard_map/pallas_call | solution.py:154
  2.6 24.1 %all_to_all.20 = bf16[8,8,896]{2,1,0:T(8,128)(2,1)S(1)} all-to-all(bf16[8,8,896]{2,1,0:T(8,128)(2,1)} %get-tuple-element.11), channel_id=1, replica_groups=mesh['zh'=4,'x'=4,'e'=8,'y'=4,'c'=2] {'e'}, dimensions={0} | all-to-all | bytes 229376 | tf_op jit(solution)/shard_map/all_to_all | solution.py:170
  26.7 0.1 broadcast_in_dim.16
  26.9 0.0 copy-start.4
  26.9 26.1 %all_to_all.21.own = bf16[16,64,768]{2,1,0:T(8,128)(2,1)S(1)} all-to-all(bf16[16,64,768]{2,1,0:T(8,128)(2,1)S(1)} %broadcast_in_dim.16), channel_id=1, replica_groups=mesh['zh'=4,'x'=4,'e'=8,'y'=4,'c'=2] {'y','x'}, dimensions={0} | all-to-all | bytes 3145728 | tf_op jit(solution)/shard_map/all_to_all | solution.py:175
  53.0 1.9 %collective-permute-start = (bf16[16,64,768]{2,1,0:T(8,128)(2,1)S(1)}, bf16[16,64,768]{2,1,0:T(8,128)(2,1)S(1)}, u32[]{:S(2)}, u32[]{:S(2)}) collective-permute-start(bf16[16,64,768]{2,1,0:T(8,128)(2,1)S(1)} %all_to_all.21.own), channel_id=1, source_target_pairs={{0,1},{1,0},{2,3},{3,2},{4,5},{5,4},{6,7},{7,6},{8,9},{9,8},{10,11... | collective-permute-start | bytes 4718600 | tf_op jit(solution)/shard_map/ppermute | solution.py:182
  54.9 3.4 %collective-permute-done.other = bf16[16,64,768]{2,1,0:T(8,128)(2,1)S(1)} collective-permute-done((bf16[16,64,768]{2,1,0:T(8,128)(2,1)S(1)}, bf16[16,64,768]{2,1,0:T(8,128)(2,1)S(1)}, u32[]{:S(2)}, u32[]{:S(2)}) %collective-permute-start) | collective-permute-done | bytes 1572896 | tf_op jit(solution)/shard_map/ppermute | solution.py:182
  58.3 0.0 copy-done.4
  58.3 0.0 copy-start
  58.3 1.1 copy-done
  59.4 0.0 copy-start.1
  59.4 1.1 copy-done.1
  60.6 0.0 copy-start.2
  60.6 1.1 copy-done.2
  61.7 0.0 copy-start.3
  61.7 1.1 copy-done.3
  62.8 2.2 %shard_map.122 = (f32[16,112,256]{2,1,0:T(8,128)S(1)}, bf16[16,112,256]{2,1,0:T(8,128)(2,1)S(1)}, bf16[256,128]{1,0:T(8,128)(2,1)S(1)}, bf16[256,128]{1,0:T(8,128)(2,1)S(1)}, f32[256,128]{1,0:T(8,128)S(1)}) custom-call(s32[1]{0:T(128)} %bitcast.4.core, bf16[16,64,768]{2,1,0:T(8,128)(2,1)S(1)} %all_to_all.21.own, ...), custom_call_target="tpu_custom_call" | custom-call | flops 1006632960 | bytes 9437184 | tf_op jit(solution)/shard_map/pallas_call | solution.py:185
  65.1 2.0 %collective-permute-start.1 = (bf16[16,112,256]{2,1,0:T(8,128)(2,1)S(1)}, bf16[16,112,256]{2,1,0:T(8,128)(2,1)S(1)}, u32[]{:S(2)}, u32[]{:S(2)}) collective-permute-start(bf16[16,112,256]{2,1,0:T(8,128)(2,1)S(1)} %get-tuple-element.13), channel_id=1, source_target_pairs={{0,1},{1,0},{2,3},{3,2},{4,5},{5,4},{6,7},{7,6},{8,9},{9,8},{10,11... | collective-permute-start | bytes 2752520 | tf_op jit(solution)/shard_map/ppermute | solution.py:213
  67.2 2.3 %collective-permute-done.1 = bf16[16,112,256]{2,1,0:T(8,128)(2,1)S(1)} collective-permute-done((bf16[16,112,256]{2,1,0:T(8,128)(2,1)S(1)}, bf16[16,112,256]{2,1,0:T(8,128)(2,1)S(1)}, u32[]{:S(2)}, u32[]{:S(2)}) %collective-permute-start.1) | collective-permute-done | bytes 917536 | tf_op jit(solution)/shard_map/ppermute | solution.py:213
  69.5 1.2 add_convert_fusion
  70.7 5.8 %all-to-all-start.2 = ((bf16[16,112,256]{2,1,0:T(8,128)(2,1)}), bf16[16,112,256]{2,1,0:T(8,128)(2,1)S(1)}, u32[]{:S(2)}, u32[]{:S(2)}) async-start(bf16[16,112,256]{2,1,0:T(8,128)(2,1)} %add_convert_fusion), calls=%async_computation.2 | async-start | bytes 1835008 | tf_op jit(solution)/shard_map/all_to_all | solution.py:214
  76.5 15.5 %all-to-all-done.2 = bf16[16,112,256]{2,1,0:T(8,128)(2,1)S(1)} async-done(((bf16[16,112,256]{2,1,0:T(8,128)(2,1)}), bf16[16,112,256]{2,1,0:T(8,128)(2,1)S(1)}, u32[]{:S(2)}, u32[]{:S(2)}) %all-to-all-start.2) | async-done | bytes 917536 | tf_op jit(solution)/shard_map/all_to_all | solution.py:214
  92.0 0.1 convert_reduce_fusion
  92.2 0.0 copy-start.5
  92.2 15.9 %collective-permute-start.3 = (bf16[40,256]{1,0:T(8,128)(2,1)S(1)}, bf16[40,256]{1,0:T(8,128)(2,1)S(1)}, u32[]{:S(2)}, u32[]{:S(2)}) collective-permute-start(bf16[40,256]{1,0:T(8,128)(2,1)S(1)} %get-tuple-element.20), channel_id=1, source_target_pairs={{0,256},{256,512},{512,768},{768,0},{1,257},{257,513},{513,769},{7... | collective-permute-start | bytes 61448 | tf_op jit(solution)/shard_map/ppermute | solution.py:225
  108.1 1.9 %collective-permute-start.2 = (bf16[40,256]{1,0:T(8,128)(2,1)S(1)}, bf16[40,256]{1,0:T(8,128)(2,1)S(1)}, u32[]{:S(2)}, u32[]{:S(2)}) collective-permute-start(bf16[40,256]{1,0:T(8,128)(2,1)S(1)} %get-tuple-element.19), channel_id=1, source_target_pairs={{0,768},{256,0},{512,256},{768,512},{1,769},{257,1},{513,257},{769... | collective-permute-start | bytes 61448 | tf_op jit(solution)/shard_map/ppermute | solution.py:225
  110.0 0.0 collective-permute-done.3
  110.1 12.6 %collective-permute-start.4 = (bf16[40,256]{1,0:T(8,128)(2,1)S(1)}, bf16[40,256]{1,0:T(8,128)(2,1)S(1)}, u32[]{:S(2)}, u32[]{:S(2)}) collective-permute-start(bf16[40,256]{1,0:T(8,128)(2,1)S(1)} %pad_maximum_fusion.2), channel_id=1, source_target_pairs={{0,256},{256,512},{512,768},{768,0},{1,257},{257,513},{513,769},{7... | collective-permute-start | bytes 61448 | tf_op jit(solution)/shard_map/ppermute | solution.py:225
  122.8 0.8 convolution_bitcast_fusion.1
  123.6 0.0 collective-permute-done.2
  123.6 0.9 collective-permute-done.4
  124.5 0.1 reshape.42
  124.6 0.7 reshape.43
  125.3 5.6 %all-to-all-start.3 = ((f32[8,6,128]{2,1,0:T(8,128)}), f32[8,6,128]{2,1,0:T(8,128)S(1)}, u32[]{:S(2)}, u32[]{:S(2)}) async-start(f32[8,6,128]{2,1,0:T(8,128)} %reshape.43), calls=%async_computation.3 | async-start | bytes 65536 | tf_op jit(solution)/shard_map/all_to_all | solution.py:236
  131.0 0.1 copy.18
  131.1 0.9 convolution_bitcast_fusion
  132.0 9.6 %all-to-all-done.3 = f32[8,6,128]{2,1,0:T(8,128)S(1)} async-done(((f32[8,6,128]{2,1,0:T(8,128)}), f32[8,6,128]{2,1,0:T(8,128)S(1)}, u32[]{:S(2)}, u32[]{:S(2)}) %all-to-all-start.3) | async-done | bytes 24608 | tf_op jit(solution)/shard_map/all_to_all | solution.py:236
  141.6 0.1 reshape.44
  141.7 0.1 reshape.45
  141.8 0.0 copy-done.5
  141.8 0.8 convolution_convert_fusion
  (18 shorter events, 0.2 us)
Async XLA Ops:
  26.9 31.4 %copy-start.4 = (bf16[1,128,128]{2,1,0:T(8,128)(2,1)S(1)}, bf16[1,128,128]{2,1,0:T(8,128)(2,1)}, u32[]{:S(2)}) copy-start(bf16[1,128,128]{2,1,0:T(8,128)(2,1)} %param.18) | copy-start | bytes 98308
  53.0 5.3 %collective-permute-start = (bf16[16,64,768]{2,1,0:T(8,128)(2,1)S(1)}, bf16[16,64,768]{2,1,0:T(8,128)(2,1)S(1)}, u32[]{:S(2)}, u32[]{:S(2)}) collective-permute-start(bf16[16,64,768]{2,1,0:T(8,128)(2,1)S(1)} %all_to_all.21.own), channel_id=1, source_target_pairs={{0,1},{1,0},{2,3},{3,2},{4,5},{5,4},{6,7},{7,6},{8,9},{9,8},{10,11... | collective-permute-start | bytes 4718600 | tf_op jit(solution)/shard_map/ppermute | solution.py:182
  58.3 1.1 copy-start
  59.4 1.1 copy-start.1
  60.6 1.1 copy-start.2
  61.7 1.1 copy-start.3
  65.1 4.4 %collective-permute-start.1 = (bf16[16,112,256]{2,1,0:T(8,128)(2,1)S(1)}, bf16[16,112,256]{2,1,0:T(8,128)(2,1)S(1)}, u32[]{:S(2)}, u32[]{:S(2)}) collective-permute-start(bf16[16,112,256]{2,1,0:T(8,128)(2,1)S(1)} %get-tuple-element.13), channel_id=1, source_target_pairs={{0,1},{1,0},{2,3},{3,2},{4,5},{5,4},{6,7},{7,6},{8,9},{9,8},{10,11... | collective-permute-start | bytes 2752520 | tf_op jit(solution)/shard_map/ppermute | solution.py:213
  70.7 21.3 %all-to-all-start.2 = ((bf16[16,112,256]{2,1,0:T(8,128)(2,1)}), bf16[16,112,256]{2,1,0:T(8,128)(2,1)S(1)}, u32[]{:S(2)}, u32[]{:S(2)}) async-start(bf16[16,112,256]{2,1,0:T(8,128)(2,1)} %add_convert_fusion), calls=%async_computation.2 | async-start | bytes 1835008 | tf_op jit(solution)/shard_map/all_to_all | solution.py:214
  92.2 49.6 %copy-start.5 = (f32[256,96]{1,0:T(8,128)S(1)}, f32[256,96]{1,0:T(8,128)}, u32[]{:S(2)}) copy-start(f32[256,96]{1,0:T(8,128)} %get-tuple-element.10) | copy-start | bytes 294916
  92.2 17.8 %collective-permute-start.3 = (bf16[40,256]{1,0:T(8,128)(2,1)S(1)}, bf16[40,256]{1,0:T(8,128)(2,1)S(1)}, u32[]{:S(2)}, u32[]{:S(2)}) collective-permute-start(bf16[40,256]{1,0:T(8,128)(2,1)S(1)} %get-tuple-element.20), channel_id=1, source_target_pairs={{0,256},{256,512},{512,768},{768,0},{1,257},{257,513},{513,769},{7... | collective-permute-start | bytes 61448 | tf_op jit(solution)/shard_map/ppermute | solution.py:225
  108.1 15.5 %collective-permute-start.2 = (bf16[40,256]{1,0:T(8,128)(2,1)S(1)}, bf16[40,256]{1,0:T(8,128)(2,1)S(1)}, u32[]{:S(2)}, u32[]{:S(2)}) collective-permute-start(bf16[40,256]{1,0:T(8,128)(2,1)S(1)} %get-tuple-element.19), channel_id=1, source_target_pairs={{0,768},{256,0},{512,256},{768,512},{1,769},{257,1},{513,257},{769... | collective-permute-start | bytes 61448 | tf_op jit(solution)/shard_map/ppermute | solution.py:225
  110.1 14.4 %collective-permute-start.4 = (bf16[40,256]{1,0:T(8,128)(2,1)S(1)}, bf16[40,256]{1,0:T(8,128)(2,1)S(1)}, u32[]{:S(2)}, u32[]{:S(2)}) collective-permute-start(bf16[40,256]{1,0:T(8,128)(2,1)S(1)} %pad_maximum_fusion.2), channel_id=1, source_target_pairs={{0,256},{256,512},{512,768},{768,0},{1,257},{257,513},{513,769},{7... | collective-permute-start | bytes 61448 | tf_op jit(solution)/shard_map/ppermute | solution.py:225
  125.3 16.3 %all-to-all-start.3 = ((f32[8,6,128]{2,1,0:T(8,128)}), f32[8,6,128]{2,1,0:T(8,128)S(1)}, u32[]{:S(2)}, u32[]{:S(2)}) async-start(f32[8,6,128]{2,1,0:T(8,128)} %reshape.43), calls=%async_computation.3 | async-start | bytes 65536 | tf_op jit(solution)/shard_map/all_to_all | solution.py:236

commit v5 on v4

--- a/solution.py
+++ b/solution.py
@@ -52,7 +52,7 @@
 
 
 def expert_kernel(
-    sizes, core, own, other, held_marks, gate_mat, up_mat, down_mat, first, second,
+    sizes, core, own, other, held_marks, ahead_mat, behind_mat, first,
     keep, give, hidden_out, down_out, flags_out, terms,
 ):
     nz, nx, ny, nc, ne = sizes
@@ -60,7 +60,7 @@
     mine = core[0]
     quarter_rows, width = own.shape[1], own.shape[2] // 2
     slots = nx * quarter_rows
-    features = gate_mat.shape[0]
+    features, units = ahead_mat.shape[0], ahead_mat.shape[1] // 2
     part, piece = features // nz, features // (nz * nxy * nc)
     low_width = first.shape[1]
 
@@ -69,13 +69,10 @@
         for ref, at_core in ((own, mine), (other, 1 - mine)):
             at = pl.multiple_of((y * nc + at_core) * width, 128)
             both = ref[y * nx : (y + 1) * nx].reshape(slots, 2 * width)
-            mats = jnp.concatenate([gate_mat[pl.ds(at, width), :], up_mat[pl.ds(at, width), :]], 1)
-            ahead = dot(both[:, :width], mats, 1, 0)
-            mats = jnp.concatenate([down_mat[:, pl.ds(at, width)], second[:, pl.ds(at, width)]], 0)
-            behind = dot(both[:, width:], mats, 1, 1)
+            ahead = dot(both[:, :width], ahead_mat[pl.ds(at, width), :], 1, 0)
+            behind = dot(both[:, width:], behind_mat[:, pl.ds(at, width)], 1, 1)
             forward = ahead if forward is None else forward + ahead
             backward = behind if backward is None else backward + behind
-    units = gate_mat.shape[1]
     gate_acc, up_acc = forward[:, :units], forward[:, units:]
     back_acc, low_back = backward[:, :units], backward[:, units:]
 
@@ -108,8 +105,7 @@
     grads = jnp.concatenate([grads[at : at + size] for at in starts], 0).astype(BF)
     for z in range(nz):
         at = slice(z * part, (z + 1) * part)
-        mats = jnp.concatenate([gate_mat[at, :], up_mat[at, :]], 1)
-        terms[at, :] = dot(mats, grads, 1, 1)
+        terms[at, :] = dot(ahead_mat[at, :], grads, 1, 1)
 
     rank_of = lax.broadcasted_iota(jnp.int32, (RANK, low_width), 1) % RANK
     fold = (rank_of == lax.broadcasted_iota(jnp.int32, (RANK, low_width), 0)).astype(BF)
@@ -179,7 +175,10 @@
         concat_axis=0,
         tiled=True,
     )
+    own, *mats = lax.optimization_barrier((own, gate_mat, up_mat, down_mat, second))
     other = lax.ppermute(own, "c", swap)
+    ahead_mat = jnp.concatenate(mats[:2], axis=1)
+    behind_mat = jnp.concatenate(mats[2:], axis=0)
     units, low_width = gate_mat.shape[1], first.shape[1]
     tall = nz * piece + RANK
     keep, give, hidden, down_coef, flags = pl.pallas_call(
@@ -191,7 +190,7 @@
             jax.ShapeDtypeStruct((slots, low_width), BF),
             jax.ShapeDtypeStruct((slots, low_width), F32),
         ),
-        in_specs=[in_smem] + [in_vmem] * 8,
+        in_specs=[in_smem] + [in_vmem] * 6,
         out_specs=(in_vmem,) * 5,
         scratch_shapes=[pltpu.VMEM((features, slots), F32)],
         compiler_params=pltpu.CompilerParams(vmem_limit_bytes=40 << 20),
@@ -203,11 +202,9 @@
         own,
         other,
         held[:, 2 * width :],
-        gate_mat,
-        up_mat,
-        down_mat,
+        ahead_mat,
+        behind_mat,
         first,
-        second,
     )
     grad_a = dot(hidden, down_coef, 0, 0)
     pair = (keep + lax.ppermute(give, "c", swap).astype(F32)).astype(BF)

time: 143 us -> 138 us (0.965)
  local copies, waits for them, and re-layouts: 5.86 us -> 1.49 us
  waiting for transfers between devices: 31.7 us -> 29.8 us
  other arithmetic: 1.42 us -> 3.12 us
    unnamed x12 -> x8, local copies, waits for them, and re-layouts: 4.54 us -> 0.17 us
    ppermute x1, waiting for transfers between devices: 3.36 us -> 1.41 us  [on_device(): other = lax.ppermute(own, 'c', swap)]
    concatenate x0 -> x2, other arithmetic: none -> 1.76 us  [the longest x1 1.66 us: on_device(): ahead_mat = jnp.concatenate(mats[:2], axis=1)]
  transfers between devices with their start and end apart: 7 -> 7, of which waited for: 5 -> 5; matrix products, arithmetic and copies ran while one was open for 1% -> 3% of each run, Pallas kernels for 0% -> 0%
where the time goes in v5:
time: 138 us
  blocking collectives  50.2 us (36%)
  starting transfers between devices  45.7 us (33%)
  waiting for transfers between devices  29.8 us (22%)
  Pallas kernels  4.21 us (3%)
  other arithmetic  3.12 us (2%)
  matrix products  2.51 us (2%)
  local copies, waits for them, and re-layouts  1.49 us (1%)
    ppermute x3, starting transfers between devices, pass_on(): lax.ppermute(sent, 'zh', [(i, (i + step) % nz) for i in range(nz)])  30.3 us
    all_to_all x1, blocking collectives, on_device(): lax.all_to_all(jnp.broadcast_to(block[None], (nxy, quarter_rows, 2 * widt...  26.1 us
    all_to_all x1, blocking collectives, on_device(): held = lax.all_to_all(send, 'e', split_axis=0, concat_axis=0, tiled=True)  24.1 us
    all_to_all x1, waiting for transfers between devices, on_device(): lax.all_to_all(pair, ('x', 'y'), split_axis=0, concat_axis=0, tiled=True)  15.5 us
    all_to_all x1, waiting for transfers between devices, on_device(): lax.all_to_all(feats.reshape(ne, piece * CAP // lanes, lanes), 'e', split...  9.61 us
    all_to_all x1, starting transfers between devices, on_device(): lax.all_to_all(pair, ('x', 'y'), split_axis=0, concat_axis=0, tiled=True)  5.8 us
    all_to_all x1, starting transfers between devices, on_device(): lax.all_to_all(feats.reshape(ne, piece * CAP // lanes, lanes), 'e', split...  5.63 us
  transfers between devices with their start and end apart: 7, of which 5 were waited for; matrix products, arithmetic and copies ran while one was open for 3% of the time, Pallas kernels for 0%

profile of v5, /device:TPU:8, one launch (start us, length us, event | category | flops | bytes accessed | tf_op | source)
XLA Modules:
  0.0 137.8 jit_solution(17106084496999820918)
XLA Ops:
  0.6 2.0 %shard_map.121 = (bf16[8,8,896]{2,1,0:T(8,128)(2,1)}, f32[256,96]{1,0:T(8,128)}) custom-call(s32[1]{0:T(128)} %bitcast.where, s32[2,96]{1,0:T(2,128)} %bitcast.55, bf16[2,96]{1,0:T(2,128)(2,1)} %bitcast.56, s32[1,96]{1,0:T(1,128)} %bitcast.57, bf16[96,384]{1,0:T(8,128)(2,1)} %tokens.1, bf16[96,384]{1,0:T(8,128)(2,1)} %cotangent.1), custom_call_target="tpu_custom_call" | custom-call | tf_op jit(solution)/shard_map/pallas_call | solution.py:150
  2.6 24.1 %all_to_all.20 = bf16[8,8,896]{2,1,0:T(8,128)(2,1)S(1)} all-to-all(bf16[8,8,896]{2,1,0:T(8,128)(2,1)} %get-tuple-element.16), channel_id=1, replica_groups=mesh['zh'=4,'x'=4,'e'=8,'y'=4,'c'=2] {'e'}, dimensions={0} | all-to-all | bytes 229376 | tf_op jit(solution)/shard_map/all_to_all | solution.py:166
  26.7 0.1 broadcast_in_dim.16
  26.9 26.1 %all_to_all.21.own = bf16[16,64,768]{2,1,0:T(8,128)(2,1)S(1)} all-to-all(bf16[16,64,768]{2,1,0:T(8,128)(2,1)S(1)} %broadcast_in_dim.16), channel_id=1, replica_groups=mesh['zh'=4,'x'=4,'e'=8,'y'=4,'c'=2] {'y','x'}, dimensions={0} | all-to-all | bytes 3145728 | tf_op jit(solution)/shard_map/all_to_all | solution.py:171
  53.0 1.9 %collective-permute-start = (bf16[16,64,768]{2,1,0:T(8,128)(2,1)S(1)}, bf16[16,64,768]{2,1,0:T(8,128)(2,1)S(1)}, u32[]{:S(2)}, u32[]{:S(2)}) collective-permute-start(bf16[16,64,768]{2,1,0:T(8,128)(2,1)S(1)} %all_to_all.21.own), channel_id=1, source_target_pairs={{0,1},{1,0},{2,3},{3,2},{4,5},{5,4},{6,7},{7,6},{8,9},{9,8},{10,11... | collective-permute-start | bytes 4718600 | tf_op jit(solution)/shard_map/ppermute | solution.py:179
  54.9 0.0 copy-start.1
  54.9 0.0 copy-start.2
  55.0 1.7 %pad_maximum_fusion.ahead_mat = bf16[3072,256]{1,0:T(8,128)(2,1)S(1)} fusion(bf16[3072,128]{1,0:T(8,128)(2,1)} %bitcast.43, bf16[3072,128]{1,0:T(8,128)(2,1)} %bitcast.44), kind=kLoop, calls=%fused_computation.2 | loop fusion | flops 3145728 | bytes 3145728 | tf_op jit(solution)/shard_map/concatenate | solution.py:180
  56.6 0.0 copy-done.1
  56.6 0.2 copy-done.2
  56.8 0.0 copy-start
  56.8 0.1 pad_maximum_fusion.1.behind_mat
  56.9 1.4 %collective-permute-done.other = bf16[16,64,768]{2,1,0:T(8,128)(2,1)S(1)} collective-permute-done((bf16[16,64,768]{2,1,0:T(8,128)(2,1)S(1)}, bf16[16,64,768]{2,1,0:T(8,128)(2,1)S(1)}, u32[]{:S(2)}, u32[]{:S(2)}) %collective-permute-start) | collective-permute-done | bytes 1572896 | tf_op jit(solution)/shard_map/ppermute | solution.py:179
  58.3 0.0 copy-done
  58.3 2.2 %shard_map.122 = (f32[16,112,256]{2,1,0:T(8,128)S(1)}, bf16[16,112,256]{2,1,0:T(8,128)(2,1)S(1)}, bf16[256,128]{1,0:T(8,128)(2,1)S(1)}, bf16[256,128]{1,0:T(8,128)(2,1)S(1)}, f32[256,128]{1,0:T(8,128)S(1)}) custom-call(s32[1]{0:T(128)} %bitcast.4.core, bf16[16,64,768]{2,1,0:T(8,128)(2,1)S(1)} %all_to_all.21.own, ...), custom_call_target="tpu_custom_call" | custom-call | flops 1006632960 | bytes 9437184 | tf_op jit(solution)/shard_map/pallas_call | solution.py:184
  60.5 2.0 %collective-permute-start.1 = (bf16[16,112,256]{2,1,0:T(8,128)(2,1)S(1)}, bf16[16,112,256]{2,1,0:T(8,128)(2,1)S(1)}, u32[]{:S(2)}, u32[]{:S(2)}) collective-permute-start(bf16[16,112,256]{2,1,0:T(8,128)(2,1)S(1)} %get-tuple-element.23), channel_id=1, source_target_pairs={{0,1},{1,0},{2,3},{3,2},{4,5},{5,4},{6,7},{7,6},{8,9},{9,8},{10,11... | collective-permute-start | bytes 2752520 | tf_op jit(solution)/shard_map/ppermute | solution.py:210
  62.6 2.3 %collective-permute-done.1 = bf16[16,112,256]{2,1,0:T(8,128)(2,1)S(1)} collective-permute-done((bf16[16,112,256]{2,1,0:T(8,128)(2,1)S(1)}, bf16[16,112,256]{2,1,0:T(8,128)(2,1)S(1)}, u32[]{:S(2)}, u32[]{:S(2)}) %collective-permute-start.1) | collective-permute-done | bytes 917536 | tf_op jit(solution)/shard_map/ppermute | solution.py:210
  64.9 1.2 add_convert_fusion
  66.1 5.8 %all-to-all-start.2 = ((bf16[16,112,256]{2,1,0:T(8,128)(2,1)}), bf16[16,112,256]{2,1,0:T(8,128)(2,1)S(1)}, u32[]{:S(2)}, u32[]{:S(2)}) async-start(bf16[16,112,256]{2,1,0:T(8,128)(2,1)} %add_convert_fusion), calls=%async_computation.2 | async-start | bytes 1835008 | tf_op jit(solution)/shard_map/all_to_all | solution.py:211
  71.9 15.5 %all-to-all-done.2 = bf16[16,112,256]{2,1,0:T(8,128)(2,1)S(1)} async-done(((bf16[16,112,256]{2,1,0:T(8,128)(2,1)}), bf16[16,112,256]{2,1,0:T(8,128)(2,1)S(1)}, u32[]{:S(2)}, u32[]{:S(2)}) %all-to-all-start.2) | async-done | bytes 917536 | tf_op jit(solution)/shard_map/all_to_all | solution.py:211
  87.4 0.1 convert_reduce_fusion
  87.6 15.7 %collective-permute-start.3 = (bf16[40,256]{1,0:T(8,128)(2,1)S(1)}, bf16[40,256]{1,0:T(8,128)(2,1)S(1)}, u32[]{:S(2)}, u32[]{:S(2)}) collective-permute-start(bf16[40,256]{1,0:T(8,128)(2,1)S(1)} %get-tuple-element.30), channel_id=1, source_target_pairs={{0,256},{256,512},{512,768},{768,0},{1,257},{257,513},{513,769},{7... | collective-permute-start | bytes 61448 | tf_op jit(solution)/shard_map/ppermute | solution.py:222
  103.3 0.0 copy-start.3
  103.4 1.9 %collective-permute-start.2 = (bf16[40,256]{1,0:T(8,128)(2,1)S(1)}, bf16[40,256]{1,0:T(8,128)(2,1)S(1)}, u32[]{:S(2)}, u32[]{:S(2)}) collective-permute-start(bf16[40,256]{1,0:T(8,128)(2,1)S(1)} %get-tuple-element.29), channel_id=1, source_target_pairs={{0,768},{256,0},{512,256},{768,512},{1,769},{257,1},{513,257},{769... | collective-permute-start | bytes 61448 | tf_op jit(solution)/shard_map/ppermute | solution.py:222
  105.3 0.0 collective-permute-done.3
  105.4 12.6 %collective-permute-start.4 = (bf16[40,256]{1,0:T(8,128)(2,1)S(1)}, bf16[40,256]{1,0:T(8,128)(2,1)S(1)}, u32[]{:S(2)}, u32[]{:S(2)}) collective-permute-start(bf16[40,256]{1,0:T(8,128)(2,1)S(1)} %pad_maximum_fusion.4), channel_id=1, source_target_pairs={{0,256},{256,512},{512,768},{768,0},{1,257},{257,513},{513,769},{7... | collective-permute-start | bytes 61448 | tf_op jit(solution)/shard_map/ppermute | solution.py:222
  118.0 0.8 convolution_bitcast_fusion.1
  118.8 0.0 collective-permute-done.2
  118.9 0.9 collective-permute-done.4
  119.8 0.1 reshape.42
  119.9 0.7 reshape.43
  120.6 5.6 %all-to-all-start.3 = ((f32[8,6,128]{2,1,0:T(8,128)}), f32[8,6,128]{2,1,0:T(8,128)S(1)}, u32[]{:S(2)}, u32[]{:S(2)}) async-start(f32[8,6,128]{2,1,0:T(8,128)} %reshape.43), calls=%async_computation.3 | async-start | bytes 65536 | tf_op jit(solution)/shard_map/all_to_all | solution.py:233
  126.2 0.1 copy.18
  126.3 0.9 convolution_bitcast_fusion
  127.2 9.6 %all-to-all-done.3 = f32[8,6,128]{2,1,0:T(8,128)S(1)} async-done(((f32[8,6,128]{2,1,0:T(8,128)}), f32[8,6,128]{2,1,0:T(8,128)S(1)}, u32[]{:S(2)}, u32[]{:S(2)}) %all-to-all-start.3) | async-done | bytes 24608 | tf_op jit(solution)/shard_map/all_to_all | solution.py:233
  136.9 0.1 reshape.44
  137.0 0.1 reshape.45
  137.1 0.0 copy-done.3
  137.1 0.8 convolution_convert_fusion
  (18 shorter events, 0.2 us)
Async XLA Ops:
  53.0 5.3 %collective-permute-start = (bf16[16,64,768]{2,1,0:T(8,128)(2,1)S(1)}, bf16[16,64,768]{2,1,0:T(8,128)(2,1)S(1)}, u32[]{:S(2)}, u32[]{:S(2)}) collective-permute-start(bf16[16,64,768]{2,1,0:T(8,128)(2,1)S(1)} %all_to_all.21.own), channel_id=1, source_target_pairs={{0,1},{1,0},{2,3},{3,2},{4,5},{5,4},{6,7},{7,6},{8,9},{9,8},{10,11... | collective-permute-start | bytes 4718600 | tf_op jit(solution)/shard_map/ppermute | solution.py:179
  54.9 1.7 %copy-start.1 = (bf16[1,128,3072]{2,1,0:T(8,128)(2,1)S(1)}, bf16[1,128,3072]{2,1,0:T(8,128)(2,1)}, u32[]{:S(2)}) copy-start(bf16[1,128,3072]{2,1,0:T(8,128)(2,1)} %param.19) | copy-start | bytes 2359300
  54.9 1.8 %copy-start.2 = (bf16[1,128,3072]{2,1,0:T(8,128)(2,1)S(1)}, bf16[1,128,3072]{2,1,0:T(8,128)(2,1)}, u32[]{:S(2)}) copy-start(bf16[1,128,3072]{2,1,0:T(8,128)(2,1)} %param.17) | copy-start | bytes 2359300
  56.8 1.5 %copy-start = (bf16[1,128,128]{2,1,0:T(8,128)(2,1)S(1)}, bf16[1,128,128]{2,1,0:T(8,128)(2,1)}, u32[]{:S(2)}) copy-start(bf16[1,128,128]{2,1,0:T(8,128)(2,1)} %param.18) | copy-start | bytes 98308
  60.5 4.4 %collective-permute-start.1 = (bf16[16,112,256]{2,1,0:T(8,128)(2,1)S(1)}, bf16[16,112,256]{2,1,0:T(8,128)(2,1)S(1)}, u32[]{:S(2)}, u32[]{:S(2)}) collective-permute-start(bf16[16,112,256]{2,1,0:T(8,128)(2,1)S(1)} %get-tuple-element.23), channel_id=1, source_target_pairs={{0,1},{1,0},{2,3},{3,2},{4,5},{5,4},{6,7},{7,6},{8,9},{9,8},{10,11... | collective-permute-start | bytes 2752520 | tf_op jit(solution)/shard_map/ppermute | solution.py:210
  66.1 21.3 %all-to-all-start.2 = ((bf16[16,112,256]{2,1,0:T(8,128)(2,1)}), bf16[16,112,256]{2,1,0:T(8,128)(2,1)S(1)}, u32[]{:S(2)}, u32[]{:S(2)}) async-start(bf16[16,112,256]{2,1,0:T(8,128)(2,1)} %add_convert_fusion), calls=%async_computation.2 | async-start | bytes 1835008 | tf_op jit(solution)/shard_map/all_to_all | solution.py:211
  87.6 17.7 %collective-permute-start.3 = (bf16[40,256]{1,0:T(8,128)(2,1)S(1)}, bf16[40,256]{1,0:T(8,128)(2,1)S(1)}, u32[]{:S(2)}, u32[]{:S(2)}) collective-permute-start(bf16[40,256]{1,0:T(8,128)(2,1)S(1)} %get-tuple-element.30), channel_id=1, source_target_pairs={{0,256},{256,512},{512,768},{768,0},{1,257},{257,513},{513,769},{7... | collective-permute-start | bytes 61448 | tf_op jit(solution)/shard_map/ppermute | solution.py:222
  103.3 33.7 %copy-start.3 = (f32[256,96]{1,0:T(8,128)S(1)}, f32[256,96]{1,0:T(8,128)}, u32[]{:S(2)}) copy-start(f32[256,96]{1,0:T(8,128)} %get-tuple-element.15) | copy-start | bytes 294916
  103.4 15.5 %collective-permute-start.2 = (bf16[40,256]{1,0:T(8,128)(2,1)S(1)}, bf16[40,256]{1,0:T(8,128)(2,1)S(1)}, u32[]{:S(2)}, u32[]{:S(2)}) collective-permute-start(bf16[40,256]{1,0:T(8,128)(2,1)S(1)} %get-tuple-element.29), channel_id=1, source_target_pairs={{0,768},{256,0},{512,256},{768,512},{1,769},{257,1},{513,257},{769... | collective-permute-start | bytes 61448 | tf_op jit(solution)/shard_map/ppermute | solution.py:222
  105.4 14.4 %collective-permute-start.4 = (bf16[40,256]{1,0:T(8,128)(2,1)S(1)}, bf16[40,256]{1,0:T(8,128)(2,1)S(1)}, u32[]{:S(2)}, u32[]{:S(2)}) collective-permute-start(bf16[40,256]{1,0:T(8,128)(2,1)S(1)} %pad_maximum_fusion.4), channel_id=1, source_target_pairs={{0,256},{256,512},{512,768},{768,0},{1,257},{257,513},{513,769},{7... | collective-permute-start | bytes 61448 | tf_op jit(solution)/shard_map/ppermute | solution.py:222
  120.6 16.3 %all-to-all-start.3 = ((f32[8,6,128]{2,1,0:T(8,128)}), f32[8,6,128]{2,1,0:T(8,128)S(1)}, u32[]{:S(2)}, u32[]{:S(2)}) async-start(f32[8,6,128]{2,1,0:T(8,128)} %reshape.43), calls=%async_computation.3 | async-start | bytes 65536 | tf_op jit(solution)/shard_map/all_to_all | solution.py:233

commit v6 on v5

--- a/solution.py
+++ b/solution.py
@@ -211,22 +211,21 @@
     plane = lax.all_to_all(pair, ("x", "y"), split_axis=0, concat_axis=0, tiled=True)
     plane = jnp.sum(plane.astype(F32), axis=0)
 
-    feats, low_own = plane[: nz * piece].reshape(nz, piece, slots), plane[nz * piece :]
+    blocks, low_own = plane[: nz * piece].reshape(nz, piece, slots), plane[nz * piece :]
     me_z = lax.axis_index("zh")
 
-    def block(step):
-        return lax.dynamic_index_in_dim(feats, (me_z + step) % nz, 0, keepdims=False)
-
-    def pass_on(rows, low, step):
-        sent = jnp.concatenate([rows, low], axis=0).astype(BF)
-        got = lax.ppermute(sent, "zh", [(i, (i + step) % nz) for i in range(nz)]).astype(F32)
-        return got[:piece], got[piece:]
-
-    far_rows, low_below = pass_on(block(2), low_own, 1)
-    rows_above, low_above = pass_on(block(nz - 1), low_own, nz - 1)
-    rows_below, low_far = pass_on(block(1) + far_rows, low_below, 1)
-    total = block(0) + rows_above + rows_below
-    low_all = low_own + low_above + low_below + low_far
+    def block(mask):
+        return lax.dynamic_index_in_dim(blocks, me_z ^ mask, 0, keepdims=False)
+
+    def swapped(parts, mask):
+        sent = jnp.concatenate(parts, axis=0).astype(BF)
+        return lax.ppermute(sent, "zh", [(i, i ^ mask) for i in range(nz)]).astype(F32)
+
+    got = swapped([block(1), block(2), low_own], 1)
+    pair_own, pair_far = block(0) + got[:piece], block(3) + got[piece : 2 * piece]
+    pair_low = low_own + got[2 * piece :]
+    got = swapped([pair_far, pair_low], 3)
+    total, low_all = pair_own + got[:piece], pair_low + got[piece:]
 
     lanes = 128
     feats = total.reshape(piece, ne, CAP).transpose(1, 0, 2)

time: 138 us -> 139 us (level)
  waiting for transfers between devices: 29.8 us -> 35.3 us
  starting transfers between devices: 45.7 us -> 40.5 us
    ppermute x3 -> x2, waiting for transfers between devices: 0.91 us -> 6.43 us  [swapped(): lax.ppermute(sent, 'zh', [(i, i ^ mask) for i in range(nz)]).astype(F32)]
    ppermute x3 -> x2, starting transfers between devices: 30.3 us -> 26.4 us  [swapped(): lax.ppermute(sent, 'zh', [(i, i ^ mask) for i in range(nz)]).astype(F32)]
  transfers between devices with their start and end apart: 7 -> 6, of which waited for: 5 -> 6; matrix products, arithmetic and copies ran while one was open for 3% -> 3% of each run, Pallas kernels for 0% -> 0%
where the time goes in v6:
time: 139 us; the launch traced here: 138 us
  blocking collectives  50.2 us (36%)
  starting transfers between devices  40.5 us (29%)
  waiting for transfers between devices  35.3 us (25%)
  Pallas kernels  4.21 us (3%)
  other arithmetic  3.11 us (2%)
  matrix products  2.51 us (2%)
  local copies, waits for them, and re-layouts  1.49 us (1%)
    ppermute x2, starting transfers between devices, swapped(): lax.ppermute(sent, 'zh', [(i, i ^ mask) for i in range(nz)]).astype(F32)  26.4 us
    all_to_all x1, blocking collectives, on_device(): lax.all_to_all(jnp.broadcast_to(block[None], (nxy, quarter_rows, 2 * widt...  26.1 us
    all_to_all x1, blocking collectives, on_device(): held = lax.all_to_all(send, 'e', split_axis=0, concat_axis=0, tiled=True)  24.1 us
    all_to_all x1, waiting for transfers between devices, on_device(): lax.all_to_all(pair, ('x', 'y'), split_axis=0, concat_axis=0, tiled=True)  15.5 us
    all_to_all x1, waiting for transfers between devices, on_device(): lax.all_to_all(feats.reshape(ne, piece * CAP // lanes, lanes), 'e', split...  9.61 us
    ppermute x2, waiting for transfers between devices, swapped(): lax.ppermute(sent, 'zh', [(i, i ^ mask) for i in range(nz)]).astype(F32)  6.43 us
    all_to_all x1, starting transfers between devices, on_device(): lax.all_to_all(pair, ('x', 'y'), split_axis=0, concat_axis=0, tiled=True)  5.8 us
    all_to_all x1, starting transfers between devices, on_device(): lax.all_to_all(feats.reshape(ne, piece * CAP // lanes, lanes), 'e', split...  4.33 us
  transfers between devices with their start and end apart: 6, of which 6 were waited for; matrix products, arithmetic and copies ran while one was open for 3% of the time, Pallas kernels for 0%

profile of v6, /device:TPU:8, one launch (start us, length us, event | category | flops | bytes accessed | tf_op | source)
XLA Modules:
  0.0 138.1 jit_solution(8911719157743606873)
XLA Ops:
  0.6 2.0 %shard_map.121 = (bf16[8,8,896]{2,1,0:T(8,128)(2,1)}, f32[256,96]{1,0:T(8,128)}) custom-call(s32[1]{0:T(128)} %bitcast.where, s32[2,96]{1,0:T(2,128)} %bitcast.55, bf16[2,96]{1,0:T(2,128)(2,1)} %bitcast.56, s32[1,96]{1,0:T(1,128)} %bitcast.57, bf16[96,384]{1,0:T(8,128)(2,1)} %tokens.1, bf16[96,384]{1,0:T(8,128)(2,1)} %cotangent.1), custom_call_target="tpu_custom_call" | custom-call | tf_op jit(solution)/shard_map/pallas_call | solution.py:150
  2.6 24.1 %all_to_all.20 = bf16[8,8,896]{2,1,0:T(8,128)(2,1)S(1)} all-to-all(bf16[8,8,896]{2,1,0:T(8,128)(2,1)} %get-tuple-element.16), channel_id=1, replica_groups=mesh['zh'=4,'x'=4,'e'=8,'y'=4,'c'=2] {'e'}, dimensions={0} | all-to-all | bytes 229376 | tf_op jit(solution)/shard_map/all_to_all | solution.py:166
  26.7 0.1 broadcast_in_dim.16
  26.9 26.1 %all_to_all.21.own = bf16[16,64,768]{2,1,0:T(8,128)(2,1)S(1)} all-to-all(bf16[16,64,768]{2,1,0:T(8,128)(2,1)S(1)} %broadcast_in_dim.16), channel_id=1, replica_groups=mesh['zh'=4,'x'=4,'e'=8,'y'=4,'c'=2] {'y','x'}, dimensions={0} | all-to-all | bytes 3145728 | tf_op jit(solution)/shard_map/all_to_all | solution.py:171
  53.0 1.9 %collective-permute-start = (bf16[16,64,768]{2,1,0:T(8,128)(2,1)S(1)}, bf16[16,64,768]{2,1,0:T(8,128)(2,1)S(1)}, u32[]{:S(2)}, u32[]{:S(2)}) collective-permute-start(bf16[16,64,768]{2,1,0:T(8,128)(2,1)S(1)} %all_to_all.21.own), channel_id=1, source_target_pairs={{0,1},{1,0},{2,3},{3,2},{4,5},{5,4},{6,7},{7,6},{8,9},{9,8},{10,11... | collective-permute-start | bytes 4718600 | tf_op jit(solution)/shard_map/ppermute | solution.py:179
  54.9 0.0 copy-start.1
  54.9 0.0 copy-start.2
  55.0 1.7 %pad_maximum_fusion.ahead_mat = bf16[3072,256]{1,0:T(8,128)(2,1)S(1)} fusion(bf16[3072,128]{1,0:T(8,128)(2,1)} %bitcast.43, bf16[3072,128]{1,0:T(8,128)(2,1)} %bitcast.44), kind=kLoop, calls=%fused_computation.2 | loop fusion | flops 3145728 | bytes 3145728 | tf_op jit(solution)/shard_map/concatenate | solution.py:180
  56.6 0.0 copy-done.1
  56.6 0.2 copy-done.2
  56.8 0.0 copy-start
  56.8 0.1 pad_maximum_fusion.1.behind_mat
  56.9 1.4 %collective-permute-done.other = bf16[16,64,768]{2,1,0:T(8,128)(2,1)S(1)} collective-permute-done((bf16[16,64,768]{2,1,0:T(8,128)(2,1)S(1)}, bf16[16,64,768]{2,1,0:T(8,128)(2,1)S(1)}, u32[]{:S(2)}, u32[]{:S(2)}) %collective-permute-start) | collective-permute-done | bytes 1572896 | tf_op jit(solution)/shard_map/ppermute | solution.py:179
  58.3 0.0 copy-done
  58.3 2.2 %shard_map.122 = (f32[16,112,256]{2,1,0:T(8,128)S(1)}, bf16[16,112,256]{2,1,0:T(8,128)(2,1)S(1)}, bf16[256,128]{1,0:T(8,128)(2,1)S(1)}, bf16[256,128]{1,0:T(8,128)(2,1)S(1)}, f32[256,128]{1,0:T(8,128)S(1)}) custom-call(s32[1]{0:T(128)} %bitcast.4.core, bf16[16,64,768]{2,1,0:T(8,128)(2,1)S(1)} %all_to_all.21.own, ...), custom_call_target="tpu_custom_call" | custom-call | flops 1006632960 | bytes 9437184 | tf_op jit(solution)/shard_map/pallas_call | solution.py:184
  60.5 2.0 %collective-permute-start.1 = (bf16[16,112,256]{2,1,0:T(8,128)(2,1)S(1)}, bf16[16,112,256]{2,1,0:T(8,128)(2,1)S(1)}, u32[]{:S(2)}, u32[]{:S(2)}) collective-permute-start(bf16[16,112,256]{2,1,0:T(8,128)(2,1)S(1)} %get-tuple-element.23), channel_id=1, source_target_pairs={{0,1},{1,0},{2,3},{3,2},{4,5},{5,4},{6,7},{7,6},{8,9},{9,8},{10,11... | collective-permute-start | bytes 2752520 | tf_op jit(solution)/shard_map/ppermute | solution.py:210
  62.6 2.3 %collective-permute-done.1 = bf16[16,112,256]{2,1,0:T(8,128)(2,1)S(1)} collective-permute-done((bf16[16,112,256]{2,1,0:T(8,128)(2,1)S(1)}, bf16[16,112,256]{2,1,0:T(8,128)(2,1)S(1)}, u32[]{:S(2)}, u32[]{:S(2)}) %collective-permute-start.1) | collective-permute-done | bytes 917536 | tf_op jit(solution)/shard_map/ppermute | solution.py:210
  64.9 1.2 add_convert_fusion
  66.1 5.8 %all-to-all-start.2 = ((bf16[16,112,256]{2,1,0:T(8,128)(2,1)}), bf16[16,112,256]{2,1,0:T(8,128)(2,1)S(1)}, u32[]{:S(2)}, u32[]{:S(2)}) async-start(bf16[16,112,256]{2,1,0:T(8,128)(2,1)} %add_convert_fusion), calls=%async_computation.2 | async-start | bytes 1835008 | tf_op jit(solution)/shard_map/all_to_all | solution.py:211
  71.9 15.5 %all-to-all-done.2 = bf16[16,112,256]{2,1,0:T(8,128)(2,1)S(1)} async-done(((bf16[16,112,256]{2,1,0:T(8,128)(2,1)}), bf16[16,112,256]{2,1,0:T(8,128)(2,1)S(1)}, u32[]{:S(2)}, u32[]{:S(2)}) %all-to-all-start.2) | async-done | bytes 917536 | tf_op jit(solution)/shard_map/all_to_all | solution.py:211
  87.4 0.1 convert_reduce_fusion
  87.6 15.7 %collective-permute-start.2 = (bf16[64,256]{1,0:T(8,128)(2,1)S(1)}, bf16[64,256]{1,0:T(8,128)(2,1)S(1)}, u32[]{:S(2)}, u32[]{:S(2)}) collective-permute-start(bf16[64,256]{1,0:T(8,128)(2,1)S(1)} %pad_maximum_fusion.2), channel_id=1, source_target_pairs={{0,256},{256,0},{512,768},{768,512},{1,257},{257,1},{513,769},{769... | collective-permute-start | bytes 98312 | tf_op jit(solution)/shard_map/ppermute | solution.py:222
  103.3 0.0 copy-start.3
  103.4 3.6 %collective-permute-done.2 = bf16[64,256]{1,0:T(8,128)(2,1)S(1)} collective-permute-done((bf16[64,256]{1,0:T(8,128)(2,1)S(1)}, bf16[64,256]{1,0:T(8,128)(2,1)S(1)}, u32[]{:S(2)}, u32[]{:S(2)}) %collective-permute-start.2) | collective-permute-done | bytes 32800 | tf_op jit(solution)/shard_map/ppermute | solution.py:222
  107.0 10.7 %collective-permute-start.3 = (bf16[40,256]{1,0:T(8,128)(2,1)S(1)}, bf16[40,256]{1,0:T(8,128)(2,1)S(1)}, u32[]{:S(2)}, u32[]{:S(2)}) collective-permute-start(bf16[40,256]{1,0:T(8,128)(2,1)S(1)} %pad_maximum_fusion.3), channel_id=1, source_target_pairs={{0,768},{256,512},{512,256},{768,0},{1,769},{257,513},{513,257},{7... | collective-permute-start | bytes 61448 | tf_op jit(solution)/shard_map/ppermute | solution.py:222
  117.7 0.8 convolution_bitcast_fusion.1
  118.5 2.9 %collective-permute-done.3 = bf16[40,256]{1,0:T(8,128)(2,1)S(1)} collective-permute-done((bf16[40,256]{1,0:T(8,128)(2,1)S(1)}, bf16[40,256]{1,0:T(8,128)(2,1)S(1)}, u32[]{:S(2)}, u32[]{:S(2)}) %collective-permute-start.3) | collective-permute-done | bytes 20512 | tf_op jit(solution)/shard_map/ppermute | solution.py:222
  121.4 0.1 reshape.42
  121.5 0.7 reshape.43
  122.2 4.3 %all-to-all-start.3 = ((f32[8,6,128]{2,1,0:T(8,128)}), f32[8,6,128]{2,1,0:T(8,128)S(1)}, u32[]{:S(2)}, u32[]{:S(2)}) async-start(f32[8,6,128]{2,1,0:T(8,128)} %reshape.43), calls=%async_computation.3 | async-start | bytes 65536 | tf_op jit(solution)/shard_map/all_to_all | solution.py:232
  126.5 0.1 copy.17
  126.6 0.9 convolution_bitcast_fusion
  127.5 9.6 %all-to-all-done.3 = f32[8,6,128]{2,1,0:T(8,128)S(1)} async-done(((f32[8,6,128]{2,1,0:T(8,128)}), f32[8,6,128]{2,1,0:T(8,128)S(1)}, u32[]{:S(2)}, u32[]{:S(2)}) %all-to-all-start.3) | async-done | bytes 24608 | tf_op jit(solution)/shard_map/all_to_all | solution.py:232
  137.2 0.1 reshape.44
  137.3 0.1 reshape.45
  137.4 0.0 copy-done.3
  137.4 0.8 convolution_convert_fusion
  (17 shorter events, 0.2 us)
Async XLA Ops:
  53.0 5.3 %collective-permute-start = (bf16[16,64,768]{2,1,0:T(8,128)(2,1)S(1)}, bf16[16,64,768]{2,1,0:T(8,128)(2,1)S(1)}, u32[]{:S(2)}, u32[]{:S(2)}) collective-permute-start(bf16[16,64,768]{2,1,0:T(8,128)(2,1)S(1)} %all_to_all.21.own), channel_id=1, source_target_pairs={{0,1},{1,0},{2,3},{3,2},{4,5},{5,4},{6,7},{7,6},{8,9},{9,8},{10,11... | collective-permute-start | bytes 4718600 | tf_op jit(solution)/shard_map/ppermute | solution.py:179
  54.9 1.7 %copy-start.1 = (bf16[1,128,3072]{2,1,0:T(8,128)(2,1)S(1)}, bf16[1,128,3072]{2,1,0:T(8,128)(2,1)}, u32[]{:S(2)}) copy-start(bf16[1,128,3072]{2,1,0:T(8,128)(2,1)} %param.19) | copy-start | bytes 2359300
  54.9 1.8 %copy-start.2 = (bf16[1,128,3072]{2,1,0:T(8,128)(2,1)S(1)}, bf16[1,128,3072]{2,1,0:T(8,128)(2,1)}, u32[]{:S(2)}) copy-start(bf16[1,128,3072]{2,1,0:T(8,128)(2,1)} %param.17) | copy-start | bytes 2359300
  56.8 1.5 %copy-start = (bf16[1,128,128]{2,1,0:T(8,128)(2,1)S(1)}, bf16[1,128,128]{2,1,0:T(8,128)(2,1)}, u32[]{:S(2)}) copy-start(bf16[1,128,128]{2,1,0:T(8,128)(2,1)} %param.18) | copy-start | bytes 98308
  60.5 4.4 %collective-permute-start.1 = (bf16[16,112,256]{2,1,0:T(8,128)(2,1)S(1)}, bf16[16,112,256]{2,1,0:T(8,128)(2,1)S(1)}, u32[]{:S(2)}, u32[]{:S(2)}) collective-permute-start(bf16[16,112,256]{2,1,0:T(8,128)(2,1)S(1)} %get-tuple-element.23), channel_id=1, source_target_pairs={{0,1},{1,0},{2,3},{3,2},{4,5},{5,4},{6,7},{7,6},{8,9},{9,8},{10,11... | collective-permute-start | bytes 2752520 | tf_op jit(solution)/shard_map/ppermute | solution.py:210
  66.1 21.3 %all-to-all-start.2 = ((bf16[16,112,256]{2,1,0:T(8,128)(2,1)}), bf16[16,112,256]{2,1,0:T(8,128)(2,1)S(1)}, u32[]{:S(2)}, u32[]{:S(2)}) async-start(bf16[16,112,256]{2,1,0:T(8,128)(2,1)} %add_convert_fusion), calls=%async_computation.2 | async-start | bytes 1835008 | tf_op jit(solution)/shard_map/all_to_all | solution.py:211
  87.6 19.3 %collective-permute-start.2 = (bf16[64,256]{1,0:T(8,128)(2,1)S(1)}, bf16[64,256]{1,0:T(8,128)(2,1)S(1)}, u32[]{:S(2)}, u32[]{:S(2)}) collective-permute-start(bf16[64,256]{1,0:T(8,128)(2,1)S(1)} %pad_maximum_fusion.2), channel_id=1, source_target_pairs={{0,256},{256,0},{512,768},{768,512},{1,257},{257,1},{513,769},{769... | collective-permute-start | bytes 98312 | tf_op jit(solution)/shard_map/ppermute | solution.py:222
  103.3 34.0 %copy-start.3 = (f32[256,96]{1,0:T(8,128)S(1)}, f32[256,96]{1,0:T(8,128)}, u32[]{:S(2)}) copy-start(f32[256,96]{1,0:T(8,128)} %get-tuple-element.15) | copy-start | bytes 294916
  107.0 14.4 %collective-permute-start.3 = (bf16[40,256]{1,0:T(8,128)(2,1)S(1)}, bf16[40,256]{1,0:T(8,128)(2,1)S(1)}, u32[]{:S(2)}, u32[]{:S(2)}) collective-permute-start(bf16[40,256]{1,0:T(8,128)(2,1)S(1)} %pad_maximum_fusion.3), channel_id=1, source_target_pairs={{0,768},{256,512},{512,256},{768,0},{1,769},{257,513},{513,257},{7... | collective-permute-start | bytes 61448 | tf_op jit(solution)/shard_map/ppermute | solution.py:222
  122.2 15.0 %all-to-all-start.3 = ((f32[8,6,128]{2,1,0:T(8,128)}), f32[8,6,128]{2,1,0:T(8,128)S(1)}, u32[]{:S(2)}, u32[]{:S(2)}) async-start(f32[8,6,128]{2,1,0:T(8,128)} %reshape.43), calls=%async_computation.3 | async-start | bytes 65536 | tf_op jit(solution)/shard_map/all_to_all | solution.py:232

commit v7 on v5

--- a/solution.py
+++ b/solution.py
@@ -206,10 +206,13 @@
         behind_mat,
         first,
     )
-    grad_a = dot(hidden, down_coef, 0, 0)
     pair = (keep + lax.ppermute(give, "c", swap).astype(F32)).astype(BF)
     plane = lax.all_to_all(pair, ("x", "y"), split_axis=0, concat_axis=0, tiled=True)
+    plane, hidden, down_coef, flags, own, combine = lax.optimization_barrier(
+        (plane, hidden, down_coef, flags, own, combine)
+    )
     plane = jnp.sum(plane.astype(F32), axis=0)
+    grad_a = dot(hidden, down_coef, 0, 0)
 
     feats, low_own = plane[: nz * piece].reshape(nz, piece, slots), plane[nz * piece :]
     me_z = lax.axis_index("zh")

time: 138 us -> 138 us (level)
    concatenate x1, other arithmetic: 0.1 us -> 1.59 us  [on_device(): behind_mat = jnp.concatenate(mats[2:], axis=0)]
    concatenate x1, other arithmetic: 1.66 us -> 0.17 us  [on_device(): ahead_mat = jnp.concatenate(mats[:2], axis=1)]
where the time goes in v7:
time: 138 us
  blocking collectives  50.2 us (36%)
  starting transfers between devices  45.7 us (33%)
  waiting for transfers between devices  29.7 us (22%)
  Pallas kernels  4.21 us (3%)
  other arithmetic  3.12 us (2%)
  matrix products  2.51 us (2%)
  local copies, waits for them, and re-layouts  1.56 us (1%)
    ppermute x3, starting transfers between devices, pass_on(): lax.ppermute(sent, 'zh', [(i, (i + step) % nz) for i in range(nz)])  30.3 us
    all_to_all x1, blocking collectives, on_device(): lax.all_to_all(jnp.broadcast_to(block[None], (nxy, quarter_rows, 2 * widt...  26.1 us
    all_to_all x1, blocking collectives, on_device(): held = lax.all_to_all(send, 'e', split_axis=0, concat_axis=0, tiled=True)  24.1 us
    all_to_all x1, waiting for transfers between devices, on_device(): lax.all_to_all(pair, ('x', 'y'), split_axis=0, concat_axis=0, tiled=True)  15.5 us
    all_to_all x1, waiting for transfers between devices, on_device(): lax.all_to_all(feats.reshape(ne, piece * CAP // lanes, lanes), 'e', split...  9.61 us
    all_to_all x1, starting transfers between devices, on_device(): lax.all_to_all(pair, ('x', 'y'), split_axis=0, concat_axis=0, tiled=True)  5.8 us
    all_to_all x1, starting transfers between devices, on_device(): lax.all_to_all(feats.reshape(ne, piece * CAP // lanes, lanes), 'e', split...  5.63 us
  transfers between devices with their start and end apart: 7, of which 5 were waited for; matrix products, arithmetic and copies ran while one was open for 3% of the time, Pallas kernels for 0%

profile of v7, /device:TPU:8, one launch (start us, length us, event | category | flops | bytes accessed | tf_op | source)
XLA Modules:
  0.0 137.8 jit_solution(7233503972892510516)
XLA Ops:
  0.6 2.0 %shard_map.121 = (bf16[8,8,896]{2,1,0:T(8,128)(2,1)}, f32[256,96]{1,0:T(8,128)}) custom-call(s32[1]{0:T(128)} %bitcast.1.where, s32[2,96]{1,0:T(2,128)} %bitcast.55, bf16[2,96]{1,0:T(2,128)(2,1)} %bitcast.56, s32[1,96]{1,0:T(1,128)} %bitcast.57, bf16[96,384]{1,0:T(8,128)(2,1)} %tokens.1, bf16[96,384]{1,0:T(8,128)(2,1)} %cotangent.1), custom_call_target="tpu_custom_call" | custom-call | tf_op jit(solution)/shard_map/pallas_call | solution.py:150
  2.6 24.1 %all_to_all.20 = bf16[8,8,896]{2,1,0:T(8,128)(2,1)S(1)} all-to-all(bf16[8,8,896]{2,1,0:T(8,128)(2,1)} %get-tuple-element.21), channel_id=1, replica_groups=mesh['zh'=4,'x'=4,'e'=8,'y'=4,'c'=2] {'e'}, dimensions={0} | all-to-all | bytes 229376 | tf_op jit(solution)/shard_map/all_to_all | solution.py:166
  26.7 0.1 broadcast_in_dim.16
  26.9 26.1 %all_to_all.21.own = bf16[16,64,768]{2,1,0:T(8,128)(2,1)S(1)} all-to-all(bf16[16,64,768]{2,1,0:T(8,128)(2,1)S(1)} %broadcast_in_dim.16), channel_id=1, replica_groups=mesh['zh'=4,'x'=4,'e'=8,'y'=4,'c'=2] {'y','x'}, dimensions={0} | all-to-all | bytes 3145728 | tf_op jit(solution)/shard_map/all_to_all | solution.py:171
  53.0 1.9 %collective-permute-start = (bf16[16,64,768]{2,1,0:T(8,128)(2,1)S(1)}, bf16[16,64,768]{2,1,0:T(8,128)(2,1)S(1)}, u32[]{:S(2)}, u32[]{:S(2)}) collective-permute-start(bf16[16,64,768]{2,1,0:T(8,128)(2,1)S(1)} %all_to_all.21.own), channel_id=1, source_target_pairs={{0,1},{1,0},{2,3},{3,2},{4,5},{5,4},{6,7},{7,6},{8,9},{9,8},{10,11... | collective-permute-start | bytes 4718600 | tf_op jit(solution)/shard_map/ppermute | solution.py:179
  54.9 0.0 copy-start.1
  54.9 0.0 copy-start.2
  55.0 1.6 %pad_maximum_fusion.1.behind_mat = bf16[256,3072]{1,0:T(8,128)(2,1)S(1)} fusion(bf16[128,3072]{1,0:T(8,128)(2,1)} %bitcast.43, bf16[128,3072]{1,0:T(8,128)(2,1)} %bitcast.44), kind=kLoop, calls=%fused_computation.3 | loop fusion | flops 3145728 | bytes 3145728 | tf_op jit(solution)/shard_map/concatenate | solution.py:181
  56.5 0.0 copy-done.1
  56.6 0.2 copy-done.2
  56.8 0.0 copy-start
  56.8 0.2 pad_maximum_fusion.ahead_mat
  57.0 1.3 collective-permute-done.other
  58.3 0.0 copy-done
  58.3 2.2 %shard_map.122 = (f32[16,112,256]{2,1,0:T(8,128)S(1)}, bf16[16,112,256]{2,1,0:T(8,128)(2,1)S(1)}, bf16[256,128]{1,0:T(8,128)(2,1)S(1)}, bf16[256,128]{1,0:T(8,128)(2,1)S(1)}, f32[256,128]{1,0:T(8,128)S(1)}) custom-call(s32[1]{0:T(128)} %bitcast.core, bf16[16,64,768]{2,1,0:T(8,128)(2,1)S(1)} %all_to_all.21.own, ...), custom_call_target="tpu_custom_call" | custom-call | flops 1006632960 | bytes 9437184 | tf_op jit(solution)/shard_map/pallas_call | solution.py:184
  60.5 2.0 %collective-permute-start.1 = (bf16[16,112,256]{2,1,0:T(8,128)(2,1)S(1)}, bf16[16,112,256]{2,1,0:T(8,128)(2,1)S(1)}, u32[]{:S(2)}, u32[]{:S(2)}) collective-permute-start(bf16[16,112,256]{2,1,0:T(8,128)(2,1)S(1)} %get-tuple-element.28), channel_id=1, source_target_pairs={{0,1},{1,0},{2,3},{3,2},{4,5},{5,4},{6,7},{7,6},{8,9},{9,8},{10,11... | collective-permute-start | bytes 2752520 | tf_op jit(solution)/shard_map/ppermute | solution.py:209
  62.6 2.3 %collective-permute-done.1 = bf16[16,112,256]{2,1,0:T(8,128)(2,1)S(1)} collective-permute-done((bf16[16,112,256]{2,1,0:T(8,128)(2,1)S(1)}, bf16[16,112,256]{2,1,0:T(8,128)(2,1)S(1)}, u32[]{:S(2)}, u32[]{:S(2)}) %collective-permute-start.1) | collective-permute-done | bytes 917536 | tf_op jit(solution)/shard_map/ppermute | solution.py:209
  64.9 1.2 add_convert_fusion
  66.1 5.8 %all-to-all-start.2 = ((bf16[16,112,256]{2,1,0:T(8,128)(2,1)}), bf16[16,112,256]{2,1,0:T(8,128)(2,1)S(1)}, u32[]{:S(2)}, u32[]{:S(2)}) async-start(bf16[16,112,256]{2,1,0:T(8,128)(2,1)} %add_convert_fusion), calls=%async_computation.2 | async-start | bytes 1835008 | tf_op jit(solution)/shard_map/all_to_all | solution.py:210
  71.9 15.5 %all-to-all-done.2 = bf16[16,112,256]{2,1,0:T(8,128)(2,1)S(1)} async-done(((bf16[16,112,256]{2,1,0:T(8,128)(2,1)}), bf16[16,112,256]{2,1,0:T(8,128)(2,1)S(1)}, u32[]{:S(2)}, u32[]{:S(2)}) %all-to-all-start.2) | async-done | bytes 917536 | tf_op jit(solution)/shard_map/all_to_all | solution.py:210
  87.4 0.1 convert_reduce_fusion
  87.6 15.7 %collective-permute-start.3 = (bf16[40,256]{1,0:T(8,128)(2,1)S(1)}, bf16[40,256]{1,0:T(8,128)(2,1)S(1)}, u32[]{:S(2)}, u32[]{:S(2)}) collective-permute-start(bf16[40,256]{1,0:T(8,128)(2,1)S(1)} %get-tuple-element.42), channel_id=1, source_target_pairs={{0,256},{256,512},{512,768},{768,0},{1,257},{257,513},{513,769},{7... | collective-permute-start | bytes 61448 | tf_op jit(solution)/shard_map/ppermute | solution.py:225
  103.3 1.9 %collective-permute-start.2 = (bf16[40,256]{1,0:T(8,128)(2,1)S(1)}, bf16[40,256]{1,0:T(8,128)(2,1)S(1)}, u32[]{:S(2)}, u32[]{:S(2)}) collective-permute-start(bf16[40,256]{1,0:T(8,128)(2,1)S(1)} %get-tuple-element.41), channel_id=1, source_target_pairs={{0,768},{256,0},{512,256},{768,512},{1,769},{257,1},{513,257},{769... | collective-permute-start | bytes 61448 | tf_op jit(solution)/shard_map/ppermute | solution.py:225
  105.2 0.0 copy-start.3
  105.3 0.0 collective-permute-done.3
  105.4 12.6 %collective-permute-start.4 = (bf16[40,256]{1,0:T(8,128)(2,1)S(1)}, bf16[40,256]{1,0:T(8,128)(2,1)S(1)}, u32[]{:S(2)}, u32[]{:S(2)}) collective-permute-start(bf16[40,256]{1,0:T(8,128)(2,1)S(1)} %pad_maximum_fusion.4), channel_id=1, source_target_pairs={{0,256},{256,512},{512,768},{768,0},{1,257},{257,513},{513,769},{7... | collective-permute-start | bytes 61448 | tf_op jit(solution)/shard_map/ppermute | solution.py:225
  118.0 0.8 convolution_bitcast_fusion.1
  118.8 0.0 collective-permute-done.2
  118.9 0.9 collective-permute-done.4
  119.8 0.1 reshape.42
  119.9 0.7 reshape.43
  120.6 5.6 %all-to-all-start.3 = ((f32[8,6,128]{2,1,0:T(8,128)}), f32[8,6,128]{2,1,0:T(8,128)S(1)}, u32[]{:S(2)}, u32[]{:S(2)}) async-start(f32[8,6,128]{2,1,0:T(8,128)} %reshape.43), calls=%async_computation.3 | async-start | bytes 65536 | tf_op jit(solution)/shard_map/all_to_all | solution.py:236
  126.2 0.1 copy.18
  126.3 0.9 convolution_bitcast_fusion
  127.2 9.6 %all-to-all-done.3 = f32[8,6,128]{2,1,0:T(8,128)S(1)} async-done(((f32[8,6,128]{2,1,0:T(8,128)}), f32[8,6,128]{2,1,0:T(8,128)S(1)}, u32[]{:S(2)}, u32[]{:S(2)}) %all-to-all-start.3) | async-done | bytes 24608 | tf_op jit(solution)/shard_map/all_to_all | solution.py:236
  136.9 0.1 reshape.44
  137.0 0.1 reshape.45
  137.1 0.0 copy-done.3
  137.1 0.8 convolution_convert_fusion
  (18 shorter events, 0.2 us)
Async XLA Ops:
  53.0 5.3 %collective-permute-start = (bf16[16,64,768]{2,1,0:T(8,128)(2,1)S(1)}, bf16[16,64,768]{2,1,0:T(8,128)(2,1)S(1)}, u32[]{:S(2)}, u32[]{:S(2)}) collective-permute-start(bf16[16,64,768]{2,1,0:T(8,128)(2,1)S(1)} %all_to_all.21.own), channel_id=1, source_target_pairs={{0,1},{1,0},{2,3},{3,2},{4,5},{5,4},{6,7},{7,6},{8,9},{9,8},{10,11... | collective-permute-start | bytes 4718600 | tf_op jit(solution)/shard_map/ppermute | solution.py:179
  54.9 1.6 %copy-start.1 = (bf16[1,3072,128]{2,1,0:T(8,128)(2,1)S(1)}, bf16[1,3072,128]{2,1,0:T(8,128)(2,1)}, u32[]{:S(2)}) copy-start(bf16[1,3072,128]{2,1,0:T(8,128)(2,1)} %param.16) | copy-start | bytes 2359300
  54.9 1.8 %copy-start.2 = (bf16[1,3072,128]{2,1,0:T(8,128)(2,1)S(1)}, bf16[1,3072,128]{2,1,0:T(8,128)(2,1)}, u32[]{:S(2)}) copy-start(bf16[1,3072,128]{2,1,0:T(8,128)(2,1)} %param.15) | copy-start | bytes 2359300
  56.8 1.5 %copy-start = (bf16[1,128,128]{2,1,0:T(8,128)(2,1)S(1)}, bf16[1,128,128]{2,1,0:T(8,128)(2,1)}, u32[]{:S(2)}) copy-start(bf16[1,128,128]{2,1,0:T(8,128)(2,1)} %param.18) | copy-start | bytes 98308
  60.5 4.4 %collective-permute-start.1 = (bf16[16,112,256]{2,1,0:T(8,128)(2,1)S(1)}, bf16[16,112,256]{2,1,0:T(8,128)(2,1)S(1)}, u32[]{:S(2)}, u32[]{:S(2)}) collective-permute-start(bf16[16,112,256]{2,1,0:T(8,128)(2,1)S(1)} %get-tuple-element.28), channel_id=1, source_target_pairs={{0,1},{1,0},{2,3},{3,2},{4,5},{5,4},{6,7},{7,6},{8,9},{9,8},{10,11... | collective-permute-start | bytes 2752520 | tf_op jit(solution)/shard_map/ppermute | solution.py:209
  66.1 21.3 %all-to-all-start.2 = ((bf16[16,112,256]{2,1,0:T(8,128)(2,1)}), bf16[16,112,256]{2,1,0:T(8,128)(2,1)S(1)}, u32[]{:S(2)}, u32[]{:S(2)}) async-start(bf16[16,112,256]{2,1,0:T(8,128)(2,1)} %add_convert_fusion), calls=%async_computation.2 | async-start | bytes 1835008 | tf_op jit(solution)/shard_map/all_to_all | solution.py:210
  87.6 17.7 %collective-permute-start.3 = (bf16[40,256]{1,0:T(8,128)(2,1)S(1)}, bf16[40,256]{1,0:T(8,128)(2,1)S(1)}, u32[]{:S(2)}, u32[]{:S(2)}) collective-permute-start(bf16[40,256]{1,0:T(8,128)(2,1)S(1)} %get-tuple-element.42), channel_id=1, source_target_pairs={{0,256},{256,512},{512,768},{768,0},{1,257},{257,513},{513,769},{7... | collective-permute-start | bytes 61448 | tf_op jit(solution)/shard_map/ppermute | solution.py:225
  103.3 15.5 %collective-permute-start.2 = (bf16[40,256]{1,0:T(8,128)(2,1)S(1)}, bf16[40,256]{1,0:T(8,128)(2,1)S(1)}, u32[]{:S(2)}, u32[]{:S(2)}) collective-permute-start(bf16[40,256]{1,0:T(8,128)(2,1)S(1)} %get-tuple-element.41), channel_id=1, source_target_pairs={{0,768},{256,0},{512,256},{768,512},{1,769},{257,1},{513,257},{769... | collective-permute-start | bytes 61448 | tf_op jit(solution)/shard_map/ppermute | solution.py:225
  105.2 31.8 %copy-start.3 = (f32[256,96]{1,0:T(8,128)S(1)}, f32[256,96]{1,0:T(8,128)}, u32[]{:S(2)}) copy-start(f32[256,96]{1,0:T(8,128)} %get-tuple-element.33) | copy-start | bytes 294916
  105.4 14.4 %collective-permute-start.4 = (bf16[40,256]{1,0:T(8,128)(2,1)S(1)}, bf16[40,256]{1,0:T(8,128)(2,1)S(1)}, u32[]{:S(2)}, u32[]{:S(2)}) collective-permute-start(bf16[40,256]{1,0:T(8,128)(2,1)S(1)} %pad_maximum_fusion.4), channel_id=1, source_target_pairs={{0,256},{256,512},{512,768},{768,0},{1,257},{257,513},{513,769},{7... | collective-permute-start | bytes 61448 | tf_op jit(solution)/shard_map/ppermute | solution.py:225
  120.6 16.3 %all-to-all-start.3 = ((f32[8,6,128]{2,1,0:T(8,128)}), f32[8,6,128]{2,1,0:T(8,128)S(1)}, u32[]{:S(2)}, u32[]{:S(2)}) async-start(f32[8,6,128]{2,1,0:T(8,128)} %reshape.43), calls=%async_computation.3 | async-start | bytes 65536 | tf_op jit(solution)/shard_map/all_to_all | solution.py:236

commit v8 on v7

--- a/solution.py
+++ b/solution.py
@@ -121,6 +121,11 @@
             out[p] = jnp.concatenate(chunks, 0).astype(out.dtype)
 
 
+def add_kernel(kept, came, pair):
+    for p in range(kept.shape[0]):
+        pair[p] = (kept[p] + came[p].astype(F32)).astype(BF)
+
+
 def on_device(
     tokens,
     cotangent,
@@ -206,7 +211,13 @@
         behind_mat,
         first,
     )
-    pair = (keep + lax.ppermute(give, "c", swap).astype(F32)).astype(BF)
+    pair = pl.pallas_call(
+        add_kernel,
+        out_shape=jax.ShapeDtypeStruct(give.shape, BF),
+        in_specs=[in_vmem] * 2,
+        out_specs=in_vmem,
+        compiler_params=pltpu.CompilerParams(vmem_limit_bytes=40 << 20),
+    )(keep, lax.ppermute(give, "c", swap))
     plane = lax.all_to_all(pair, ("x", "y"), split_axis=0, concat_axis=0, tiled=True)
     plane, hidden, down_coef, flags, own, combine = lax.optimization_barrier(
         (plane, hidden, down_coef, flags, own, combine)

time: 138 us -> 138 us (level)
  no operation moved by 1% of the time
where the time goes in v8:
time: 138 us
  blocking collectives  50.2 us (36%)
  starting transfers between devices  45.7 us (33%)
  waiting for transfers between devices  29.7 us (22%)
  Pallas kernels  5.29 us (4%)
  matrix products  2.51 us (2%)
  other arithmetic  1.94 us (1%)
  local copies, waits for them, and re-layouts  1.56 us (1%)
    ppermute x3, starting transfers between devices, pass_on(): lax.ppermute(sent, 'zh', [(i, (i + step) % nz) for i in range(nz)])  30.3 us
    all_to_all x1, blocking collectives, on_device(): lax.all_to_all(jnp.broadcast_to(block[None], (nxy, quarter_rows, 2 * widt...  26.1 us
    all_to_all x1, blocking collectives, on_device(): held = lax.all_to_all(send, 'e', split_axis=0, concat_axis=0, tiled=True)  24.1 us
    all_to_all x1, waiting for transfers between devices, on_device(): lax.all_to_all(pair, ('x', 'y'), split_axis=0, concat_axis=0, tiled=True)  15.5 us
    all_to_all x1, waiting for transfers between devices, on_device(): lax.all_to_all(feats.reshape(ne, piece * CAP // lanes, lanes), 'e', split...  9.61 us
    all_to_all x1, starting transfers between devices, on_device(): lax.all_to_all(pair, ('x', 'y'), split_axis=0, concat_axis=0, tiled=True)  5.8 us
    all_to_all x1, starting transfers between devices, on_device(): lax.all_to_all(feats.reshape(ne, piece * CAP // lanes, lanes), 'e', split...  5.63 us
  transfers between devices with their start and end apart: 7, of which 5 were waited for; matrix products, arithmetic and copies ran while one was open for 3% of the time, Pallas kernels for 0%

profile of v8, /device:TPU:8, one launch (start us, length us, event | category | flops | bytes accessed | tf_op | source)
XLA Modules:
  0.0 137.7 jit_solution(16406520411928694816)
XLA Ops:
  0.6 2.0 %shard_map.121 = (bf16[8,8,896]{2,1,0:T(8,128)(2,1)}, f32[256,96]{1,0:T(8,128)}) custom-call(s32[1]{0:T(128)} %bitcast.1.where, s32[2,96]{1,0:T(2,128)} %bitcast.55, bf16[2,96]{1,0:T(2,128)(2,1)} %bitcast.56, s32[1,96]{1,0:T(1,128)} %bitcast.57, bf16[96,384]{1,0:T(8,128)(2,1)} %tokens.1, bf16[96,384]{1,0:T(8,128)(2,1)} %cotangent.1), custom_call_target="tpu_custom_call" | custom-call | tf_op jit(solution)/shard_map/pallas_call | solution.py:155
  2.6 24.1 %all_to_all.20 = bf16[8,8,896]{2,1,0:T(8,128)(2,1)S(1)} all-to-all(bf16[8,8,896]{2,1,0:T(8,128)(2,1)} %get-tuple-element.21), channel_id=1, replica_groups=mesh['zh'=4,'x'=4,'e'=8,'y'=4,'c'=2] {'e'}, dimensions={0} | all-to-all | bytes 229376 | tf_op jit(solution)/shard_map/all_to_all | solution.py:171
  26.7 0.1 broadcast_in_dim.16
  26.9 26.1 %all_to_all.21.own = bf16[16,64,768]{2,1,0:T(8,128)(2,1)S(1)} all-to-all(bf16[16,64,768]{2,1,0:T(8,128)(2,1)S(1)} %broadcast_in_dim.16), channel_id=1, replica_groups=mesh['zh'=4,'x'=4,'e'=8,'y'=4,'c'=2] {'y','x'}, dimensions={0} | all-to-all | bytes 3145728 | tf_op jit(solution)/shard_map/all_to_all | solution.py:176
  53.0 1.9 %collective-permute-start = (bf16[16,64,768]{2,1,0:T(8,128)(2,1)S(1)}, bf16[16,64,768]{2,1,0:T(8,128)(2,1)S(1)}, u32[]{:S(2)}, u32[]{:S(2)}) collective-permute-start(bf16[16,64,768]{2,1,0:T(8,128)(2,1)S(1)} %all_to_all.21.own), channel_id=1, source_target_pairs={{0,1},{1,0},{2,3},{3,2},{4,5},{5,4},{6,7},{7,6},{8,9},{9,8},{10,11... | collective-permute-start | bytes 4718600 | tf_op jit(solution)/shard_map/ppermute | solution.py:184
  54.9 0.0 copy-start.1
  54.9 0.0 copy-start.2
  55.0 1.6 %pad_maximum_fusion.1.behind_mat = bf16[256,3072]{1,0:T(8,128)(2,1)S(1)} fusion(bf16[128,3072]{1,0:T(8,128)(2,1)} %bitcast.43, bf16[128,3072]{1,0:T(8,128)(2,1)} %bitcast.44), kind=kLoop, calls=%fused_computation.2 | loop fusion | flops 3145728 | bytes 3145728 | tf_op jit(solution)/shard_map/concatenate | solution.py:186
  56.5 0.0 copy-done.1
  56.6 0.2 copy-done.2
  56.8 0.0 copy-start
  56.8 0.2 pad_maximum_fusion.ahead_mat
  57.0 1.3 collective-permute-done.other
  58.3 0.0 copy-done
  58.3 2.2 %shard_map.122 = (f32[16,112,256]{2,1,0:T(8,128)S(1)}, bf16[16,112,256]{2,1,0:T(8,128)(2,1)S(1)}, bf16[256,128]{1,0:T(8,128)(2,1)S(1)}, bf16[256,128]{1,0:T(8,128)(2,1)S(1)}, f32[256,128]{1,0:T(8,128)S(1)}) custom-call(s32[1]{0:T(128)} %bitcast.core, bf16[16,64,768]{2,1,0:T(8,128)(2,1)S(1)} %all_to_all.21.own, ...), custom_call_target="tpu_custom_call" | custom-call | flops 1006632960 | bytes 9437184 | tf_op jit(solution)/shard_map/pallas_call | solution.py:189
  60.5 2.0 %collective-permute-start.1 = (bf16[16,112,256]{2,1,0:T(8,128)(2,1)S(1)}, bf16[16,112,256]{2,1,0:T(8,128)(2,1)S(1)}, u32[]{:S(2)}, u32[]{:S(2)}) collective-permute-start(bf16[16,112,256]{2,1,0:T(8,128)(2,1)S(1)} %get-tuple-element.28), channel_id=1, source_target_pairs={{0,1},{1,0},{2,3},{3,2},{4,5},{5,4},{6,7},{7,6},{8,9},{9,8},{10,11... | collective-permute-start | bytes 2752520 | tf_op jit(solution)/shard_map/ppermute | solution.py:220
  62.6 2.3 %collective-permute-done.1.came = bf16[16,112,256]{2,1,0:T(8,128)(2,1)S(1)} collective-permute-done((bf16[16,112,256]{2,1,0:T(8,128)(2,1)S(1)}, bf16[16,112,256]{2,1,0:T(8,128)(2,1)S(1)}, u32[]{:S(2)}, u32[]{:S(2)}) %collective-permute-start.1) | collective-permute-done | bytes 917536 | tf_op jit(solution)/shard_map/ppermute | solution.py:220
  64.9 1.1 shard_map.123
  66.0 5.8 %all-to-all-start.2 = ((bf16[16,112,256]{2,1,0:T(8,128)(2,1)}), bf16[16,112,256]{2,1,0:T(8,128)(2,1)S(1)}, u32[]{:S(2)}, u32[]{:S(2)}) async-start(bf16[16,112,256]{2,1,0:T(8,128)(2,1)} %shard_map.123), calls=%async_computation.2 | async-start | bytes 1835008 | tf_op jit(solution)/shard_map/all_to_all | solution.py:221
  71.8 15.5 %all-to-all-done.2 = bf16[16,112,256]{2,1,0:T(8,128)(2,1)S(1)} async-done(((bf16[16,112,256]{2,1,0:T(8,128)(2,1)}), bf16[16,112,256]{2,1,0:T(8,128)(2,1)S(1)}, u32[]{:S(2)}, u32[]{:S(2)}) %all-to-all-start.2) | async-done | bytes 917536 | tf_op jit(solution)/shard_map/all_to_all | solution.py:221
  87.3 0.1 convert_reduce_fusion
  87.5 15.7 %collective-permute-start.3 = (bf16[40,256]{1,0:T(8,128)(2,1)S(1)}, bf16[40,256]{1,0:T(8,128)(2,1)S(1)}, u32[]{:S(2)}, u32[]{:S(2)}) collective-permute-start(bf16[40,256]{1,0:T(8,128)(2,1)S(1)} %get-tuple-element.42), channel_id=1, source_target_pairs={{0,256},{256,512},{512,768},{768,0},{1,257},{257,513},{513,769},{7... | collective-permute-start | bytes 61448 | tf_op jit(solution)/shard_map/ppermute | solution.py:236
  103.2 1.9 %collective-permute-start.2 = (bf16[40,256]{1,0:T(8,128)(2,1)S(1)}, bf16[40,256]{1,0:T(8,128)(2,1)S(1)}, u32[]{:S(2)}, u32[]{:S(2)}) collective-permute-start(bf16[40,256]{1,0:T(8,128)(2,1)S(1)} %get-tuple-element.41), channel_id=1, source_target_pairs={{0,768},{256,0},{512,256},{768,512},{1,769},{257,1},{513,257},{769... | collective-permute-start | bytes 61448 | tf_op jit(solution)/shard_map/ppermute | solution.py:236
  105.1 0.0 copy-start.3
  105.2 0.0 collective-permute-done.3
  105.3 12.6 %collective-permute-start.4 = (bf16[40,256]{1,0:T(8,128)(2,1)S(1)}, bf16[40,256]{1,0:T(8,128)(2,1)S(1)}, u32[]{:S(2)}, u32[]{:S(2)}) collective-permute-start(bf16[40,256]{1,0:T(8,128)(2,1)S(1)} %pad_maximum_fusion.4), channel_id=1, source_target_pairs={{0,256},{256,512},{512,768},{768,0},{1,257},{257,513},{513,769},{7... | collective-permute-start | bytes 61448 | tf_op jit(solution)/shard_map/ppermute | solution.py:236
  117.9 0.8 convolution_bitcast_fusion.1
  118.7 0.0 collective-permute-done.2
  118.8 0.9 collective-permute-done.4
  119.7 0.1 reshape.42
  119.8 0.7 reshape.43
  120.5 5.6 %all-to-all-start.3 = ((f32[8,6,128]{2,1,0:T(8,128)}), f32[8,6,128]{2,1,0:T(8,128)S(1)}, u32[]{:S(2)}, u32[]{:S(2)}) async-start(f32[8,6,128]{2,1,0:T(8,128)} %reshape.43), calls=%async_computation.3 | async-start | bytes 65536 | tf_op jit(solution)/shard_map/all_to_all | solution.py:247
  126.1 0.1 copy.18
  126.2 0.9 convolution_bitcast_fusion
  127.1 9.6 %all-to-all-done.3 = f32[8,6,128]{2,1,0:T(8,128)S(1)} async-done(((f32[8,6,128]{2,1,0:T(8,128)}), f32[8,6,128]{2,1,0:T(8,128)S(1)}, u32[]{:S(2)}, u32[]{:S(2)}) %all-to-all-start.3) | async-done | bytes 24608 | tf_op jit(solution)/shard_map/all_to_all | solution.py:247
  136.8 0.1 reshape.44
  136.9 0.1 reshape.45
  137.0 0.0 copy-done.3
  137.0 0.8 convolution_convert_fusion
  (18 shorter events, 0.2 us)
Async XLA Ops:
  53.0 5.3 %collective-permute-start = (bf16[16,64,768]{2,1,0:T(8,128)(2,1)S(1)}, bf16[16,64,768]{2,1,0:T(8,128)(2,1)S(1)}, u32[]{:S(2)}, u32[]{:S(2)}) collective-permute-start(bf16[16,64,768]{2,1,0:T(8,128)(2,1)S(1)} %all_to_all.21.own), channel_id=1, source_target_pairs={{0,1},{1,0},{2,3},{3,2},{4,5},{5,4},{6,7},{7,6},{8,9},{9,8},{10,11... | collective-permute-start | bytes 4718600 | tf_op jit(solution)/shard_map/ppermute | solution.py:184
  54.9 1.6 %copy-start.1 = (bf16[1,3072,128]{2,1,0:T(8,128)(2,1)S(1)}, bf16[1,3072,128]{2,1,0:T(8,128)(2,1)}, u32[]{:S(2)}) copy-start(bf16[1,3072,128]{2,1,0:T(8,128)(2,1)} %param.16) | copy-start | bytes 2359300
  54.9 1.8 %copy-start.2 = (bf16[1,3072,128]{2,1,0:T(8,128)(2,1)S(1)}, bf16[1,3072,128]{2,1,0:T(8,128)(2,1)}, u32[]{:S(2)}) copy-start(bf16[1,3072,128]{2,1,0:T(8,128)(2,1)} %param.15) | copy-start | bytes 2359300
  56.8 1.5 %copy-start = (bf16[1,128,128]{2,1,0:T(8,128)(2,1)S(1)}, bf16[1,128,128]{2,1,0:T(8,128)(2,1)}, u32[]{:S(2)}) copy-start(bf16[1,128,128]{2,1,0:T(8,128)(2,1)} %param.18) | copy-start | bytes 98308
  60.5 4.4 %collective-permute-start.1 = (bf16[16,112,256]{2,1,0:T(8,128)(2,1)S(1)}, bf16[16,112,256]{2,1,0:T(8,128)(2,1)S(1)}, u32[]{:S(2)}, u32[]{:S(2)}) collective-permute-start(bf16[16,112,256]{2,1,0:T(8,128)(2,1)S(1)} %get-tuple-element.28), channel_id=1, source_target_pairs={{0,1},{1,0},{2,3},{3,2},{4,5},{5,4},{6,7},{7,6},{8,9},{9,8},{10,11... | collective-permute-start | bytes 2752520 | tf_op jit(solution)/shard_map/ppermute | solution.py:220
  66.0 21.3 %all-to-all-start.2 = ((bf16[16,112,256]{2,1,0:T(8,128)(2,1)}), bf16[16,112,256]{2,1,0:T(8,128)(2,1)S(1)}, u32[]{:S(2)}, u32[]{:S(2)}) async-start(bf16[16,112,256]{2,1,0:T(8,128)(2,1)} %shard_map.123), calls=%async_computation.2 | async-start | bytes 1835008 | tf_op jit(solution)/shard_map/all_to_all | solution.py:221
  87.5 17.7 %collective-permute-start.3 = (bf16[40,256]{1,0:T(8,128)(2,1)S(1)}, bf16[40,256]{1,0:T(8,128)(2,1)S(1)}, u32[]{:S(2)}, u32[]{:S(2)}) collective-permute-start(bf16[40,256]{1,0:T(8,128)(2,1)S(1)} %get-tuple-element.42), channel_id=1, source_target_pairs={{0,256},{256,512},{512,768},{768,0},{1,257},{257,513},{513,769},{7... | collective-permute-start | bytes 61448 | tf_op jit(solution)/shard_map/ppermute | solution.py:236
  103.2 15.5 %collective-permute-start.2 = (bf16[40,256]{1,0:T(8,128)(2,1)S(1)}, bf16[40,256]{1,0:T(8,128)(2,1)S(1)}, u32[]{:S(2)}, u32[]{:S(2)}) collective-permute-start(bf16[40,256]{1,0:T(8,128)(2,1)S(1)} %get-tuple-element.41), channel_id=1, source_target_pairs={{0,768},{256,0},{512,256},{768,512},{1,769},{257,1},{513,257},{769... | collective-permute-start | bytes 61448 | tf_op jit(solution)/shard_map/ppermute | solution.py:236
  105.1 31.8 %copy-start.3 = (f32[256,96]{1,0:T(8,128)S(1)}, f32[256,96]{1,0:T(8,128)}, u32[]{:S(2)}) copy-start(f32[256,96]{1,0:T(8,128)} %get-tuple-element.33) | copy-start | bytes 294916
  105.3 14.4 %collective-permute-start.4 = (bf16[40,256]{1,0:T(8,128)(2,1)S(1)}, bf16[40,256]{1,0:T(8,128)(2,1)S(1)}, u32[]{:S(2)}, u32[]{:S(2)}) collective-permute-start(bf16[40,256]{1,0:T(8,128)(2,1)S(1)} %pad_maximum_fusion.4), channel_id=1, source_target_pairs={{0,256},{256,512},{512,768},{768,0},{1,257},{257,513},{513,769},{7... | collective-permute-start | bytes 61448 | tf_op jit(solution)/shard_map/ppermute | solution.py:236
  120.5 16.3 %all-to-all-start.3 = ((f32[8,6,128]{2,1,0:T(8,128)}), f32[8,6,128]{2,1,0:T(8,128)S(1)}, u32[]{:S(2)}, u32[]{:S(2)}) async-start(f32[8,6,128]{2,1,0:T(8,128)} %reshape.43), calls=%async_computation.3 | async-start | bytes 65536 | tf_op jit(solution)/shard_map/all_to_all | solution.py:247
